TPU v7x, 32 devices: a whole 2x2x4 slice. The times are simulated.
32 devices in a mesh: section: 2 (over core), chan: 4 (over z), dp: 4 (over y, x).
Axes of the slice: x: 2, y: 2, z: 4, core: 2. Of those that a mesh axis runs over, the one named last changes fastest.
Arguments:
- inputs: bfloat16 [2, 16, 1024, 768], P(None, ('dp', 'chan')), may hold values from -6 to 6
- lengths: int32 [2, 16], P(None, ('dp', 'chan')), may hold values from 512 to 1024, as said below
- out_grad: bfloat16 [2, 16, 1024, 768], P(None, ('dp', 'chan')), may hold values from -6 to 6
- ln_mix_gain: bfloat16 [1, 768], P(None, 'chan'), may hold values from 0.5 to 1.5
- w_in: bfloat16 [1, 768, 2304], P(None, 'chan'), may hold values from -0.21875 to 0.21875
- short_taps: bfloat16 [1, 3, 2304], P(None, None, 'chan'), may hold values from -3 to 3
- long_taps: bfloat16 [1, 1024, 768], P(None, None, 'chan'), may hold values from -0.5 to 0.5
- w_out: bfloat16 [1, 768, 768], P(None, 'chan'), may hold values from -0.21875 to 0.21875
- ln_mlp_gain: bfloat16 [1, 768], P(None, 'chan'), may hold values from 0.5 to 1.5
- w_up: bfloat16 [1, 768, 3072], P(None, 'chan'), may hold values from -0.21875 to 0.21875
- w_down: bfloat16 [1, 3072, 768], P(None, 'chan'), may hold values from -0.109375 to 0.109375
Outputs:
- activations: bfloat16 [2, 2, 16, 1024, 768], P('section', None, ('dp', 'chan'))
- act_grads: float32 [2, 2, 16, 1024, 768], P('section', None, ('dp', 'chan'))
- grad_ln_mix_gain: float32 [1, 768], P(None, 'chan')
- grad_w_in: float32 [1, 768, 2304], P(None, 'chan')
- grad_short_taps: float32 [1, 3, 2304], P(None, None, 'chan')
- grad_long_taps: float32 [1, 1024, 768], P(None, None, 'chan')
- grad_w_out: float32 [1, 768, 768], P(None, 'chan')
- grad_ln_mlp_gain: float32 [1, 768], P(None, 'chan')
- grad_w_up: float32 [1, 768, 3072], P(None, 'chan')
- grad_w_down: float32 [1, 3072, 768], P(None, 'chan')
Inputs may be any that keep to these rules, and one draw needn't show every extreme that they name: `lengths`: in every micro-batch one slot holds 1024 live positions and another holds 512.
All inputs are finite; a program needn't handle non-finite values.
Results may differ from a plain program's by a relative error of at most 0.015.
Values may be sent and summed in bfloat16 or wider, within the bound.
No kernel may reach another device: no remote copies, remote signals or barrier semaphores. Data moves between devices by JAX's collectives and lax.ppermute only.
A program may use at most 384 MiB of HBM per device.

v0:
```python
import math

import jax
import jax.numpy as jnp
import ml_dtypes
import numpy as np
from jax import lax
from jax.experimental import pallas as pl
from jax.experimental.pallas import tpu as pltpu
from jax.sharding import PartitionSpec as P

decay_rate = 0.003
bf16 = jnp.bfloat16
f32 = jnp.float32
MIB = 1 << 20


def odd_basis(length):
    phase = (2 * np.arange(length)[:, None] + 1) * np.arange(length)[None, :] % (4 * length)
    angle = phase * (math.pi / (2 * length))
    return np.concatenate([np.cos(angle), np.sin(angle)], 0).astype(ml_dtypes.bfloat16)


def dot(a, b, ca=1, cb=0):
    return lax.dot_general(a, b, (((ca,), (cb,)), ((), ())), preferred_element_type=f32)


def norm_parts(values):
    centered = values - jnp.mean(values, axis=-1, keepdims=True)
    spread = jnp.mean(centered * centered, axis=-1, keepdims=True)
    inv = lax.rsqrt(spread + 1e-05)
    return centered * inv, inv


def norm_back(grad_normed, hat, inv, gain):
    grad_hat = grad_normed * gain
    return inv * (
        grad_hat
        - jnp.mean(grad_hat, axis=-1, keepdims=True)
        - hat * jnp.mean(grad_hat * hat, axis=-1, keepdims=True)
    )


def call(kernel, grid, in_specs, out_specs, out_shape, scratch, args, flops, nbytes, limit=56, prefetch=0):
    spec = pltpu.PrefetchScalarGridSpec(
        num_scalar_prefetch=prefetch, grid=grid, in_specs=in_specs, out_specs=out_specs, scratch_shapes=scratch
    )
    return pl.pallas_call(
        kernel,
        grid_spec=spec,
        out_shape=out_shape,
        compiler_params=pltpu.CompilerParams(
            dimension_semantics=("arbitrary",) * len(grid), vmem_limit_bytes=limit * MIB
        ),
        cost_estimate=pl.CostEstimate(flops=flops, bytes_accessed=nbytes, transcendentals=0),
    )(*args)


def whole(shape):
    return pl.BlockSpec(shape, lambda *_: (0,) * len(shape), pipeline_mode=pl.Buffered(1))


def rows_of(r, c):
    return pl.BlockSpec((r, c), lambda i, *_: (i, 0))


def cols_of(r, c, start=0):
    return pl.BlockSpec((r, c), lambda i, *_: (0, i + start))


def sds(shape, dtype):
    return jax.ShapeDtypeStruct(shape, dtype)


ANY = pl.BlockSpec(memory_space=pl.ANY)
SHIFTS = (1, 3, 2)


def start_all(copies, sems):
    for n, (a, b) in enumerate(copies):
        pltpu.make_async_copy(a, b, sems.at[n]).start()


def wait_all(copies, sems):
    for n, (a, b) in enumerate(copies):
        pltpu.make_async_copy(a, b, sems.at[n]).wait()


def sources(idx, mine, other):
    z, d, s = idx[0], idx[1], idx[2]
    for e in range(4):
        for j, k in enumerate(SHIFTS):
            for ref, side in ((mine[e], s), (other[e], 1 - s)):
                yield ref, j, lax.rem(z + 4 - k, 4), d ^ e, side


def in_copies(idx, own, mine, other, dst):
    part, half = own.shape[0], own.shape[1] // 2
    r = part // 4
    out = [(own, dst.at[pl.ds(pl.multiple_of(idx[0] * part, 16), part), :])]
    for ref, j, z, d, side in sources(idx, mine, other):
        out.append((ref.at[pl.ds(j * r, r), :],
                    dst.at[pl.ds(pl.multiple_of(z * part + d * r, 16), r), pl.ds(pl.multiple_of(side * half, 128), half)]))
    return out


def up_copies(idx, own, mine, other, dst):
    part, ff = own.shape
    c = ff // 8
    step = part + part // 4
    out = [(own, dst.at[pl.ds(pl.multiple_of(idx[0] * part, 16), part), :])]
    for ref, j, z, d, side in sources(idx, mine, other):
        out.append((ref.at[pl.ds(j * step, part), :],
                    dst.at[pl.ds(pl.multiple_of(z * part, 16), part), pl.ds(pl.multiple_of(side * 4 * c + d * c, 128), c)]))
    return out


def down_copies(idx, own, mine, other, dst):
    q, width = own.shape
    r = q // 4
    h = width // 2
    out = [(own, dst.at[pl.ds(pl.multiple_of(idx[0] * q, 16), q), :])]
    for ref, j, z, d, side in sources(idx, mine, other):
        out.append((ref.at[pl.ds(j * r, r), :],
                    dst.at[pl.ds(pl.multiple_of(z * q + d * r, 16), r), pl.ds(pl.multiple_of(side * h, 128), h)]))
    return out


def out_copies(idx, own, mine, other, dst):
    part, width = own.shape
    r = part // 4
    h = width // 2
    out = [(own, dst.at[pl.ds(pl.multiple_of(idx[0] * part, 16), part), :])]
    for ref, j, z, d, side in sources(idx, mine, other):
        out.append((ref.at[pl.ds(j * 5 * r + part, r), :],
                    dst.at[pl.ds(pl.multiple_of(z * part + d * r, 16), r), pl.ds(pl.multiple_of(side * h, 128), h)]))
    return out


def rest_copies(idx, own, mine, other, dst, start, half):
    part = own.shape[0]
    r = part // 4
    out = [(own, dst.at[pl.ds(pl.multiple_of(idx[0] * part, 16), part), :])]
    for ref, j, z, d, side in sources(idx, mine, other):
        out.append((ref.at[pl.ds(j * r, r), pl.ds(start, half)],
                    dst.at[pl.ds(pl.multiple_of(z * part + d * r, 16), r), pl.ds(pl.multiple_of(side * half, 128), half)]))
    return out


SEMS = pltpu.SemaphoreType.DMA((25,))


CH = 256


def spectra_kernel(idx, *refs):
    held, (own_taps, own_small, basis_ref, out_ref, small_ref, taps_ref, taps, small, tall, sig, sems, sems2) = refs[:8], refs[8:]
    mine, other = held[:4], held[4:]
    length = taps.shape[1]

    @pl.when(pl.program_id(0) == 0)
    def _():
        copies = rest_copies(idx, own_taps, mine, other, taps, REST_TAPS, length // 2)
        part = own_small.shape[0]
        r = part // 4
        copies2 = [(own_small, small.at[pl.ds(pl.multiple_of(idx[0] * part, 16), part), :])]
        for e in range(4):
            for j, k in enumerate(SHIFTS):
                z = lax.rem(idx[0] + 4 - k, 4)
                copies2.append((mine[e].at[pl.ds(j * r, r), pl.ds(REST_SMALL, 128)],
                                small.at[pl.ds(pl.multiple_of(z * part + (idx[1] ^ e) * r, 16), r), :]))
        start_all(copies, sems)
        start_all(copies2, sems2)
        wait_all(copies2, sems2)
        wait_all(copies, sems)
        wide = small[...].astype(f32)
        small_ref[...] = wide.T[0:8]
        for z in range(4):
            for q in range(3):
                tall[(3 * z + q) * part : (3 * z + q + 1) * part] = pltpu.roll(wide[z * part : (z + 1) * part], 126 - q, 1)
        taps_ref[...] = tall[...].T[0:8]

    position = lax.broadcasted_iota(jnp.int32, (1, length), 1).astype(f32)
    rows = pl.ds(pl.multiple_of(pl.program_id(0) * CH, CH), CH)
    sig[...] = (taps[rows, :].astype(f32) * (jnp.exp(-decay_rate * position) / length)).astype(bf16)
    out_ref[...] = dot(basis_ref[...], sig[...], 1, 1).astype(bf16)


REST_TAPS, REST_SMALL = 0, 512


def kernel_spectra(idx, rest, own_taps, own_small, basis):
    length = own_taps.shape[1]
    width = own_taps.shape[0] * 4
    return call(
        spectra_kernel,
        (width // CH,),
        [ANY] * 10 + [whole(basis.shape)],
        [cols_of(2 * length, CH), whole((8, width)), whole((8, 3 * width))],
        [sds((2 * length, width), bf16), sds((8, width), f32), sds((8, 3 * width), f32)],
        [pltpu.VMEM((width, length), bf16), pltpu.VMEM((width, 128), bf16), pltpu.VMEM((3 * width, 128), f32), pltpu.VMEM((CH, length), bf16), SEMS, SEMS],
        (idx, *rest, own_taps, own_small, basis),
        4 * length * length * width,
        basis.size * 2 + 6 * length * width,
        prefetch=1,
    )


class Mover:
    def __init__(self, sems):
        self.sems, self.used = sems, 0

    def start(self, src, dst):
        copy = pltpu.make_async_copy(src, dst, self.sems.at[self.used])
        self.used += 1
        copy.start()
        return copy

    def pieces(self, pairs):
        return [self.start(a, b) for a, b in pairs]


def settle(*copies):
    for c in copies:
        if isinstance(c, list):
            settle(*c)
        else:
            c.wait()


def manual(kernel, n_in, vmem_in, out_shapes, out_specs, scratch, sems, args, flops, nbytes):
    return call(
        kernel,
        (1,),
        [ANY] * n_in + [whole(v.shape) for v in vmem_in],
        out_specs,
        out_shapes,
        [*scratch, pltpu.SemaphoreType.DMA((sems,))],
        (*args, *vmem_in),
        flops,
        nbytes,
        limit=60,
        prefetch=1,
    )


def blocks_of(i):
    return slice(i * CH, (i + 1) * CH)


def front_kernel(idx, *refs):
    held, (own, x_in, spec_in, basis_in, back_in, gain, taps, normed_o, m_o, qkv_o, sspec_o, conv_o, gated_o,
           x_s, w_s, spec_s, basis_s, back_s, normed_s, m_s, qkv_s, sspec_s, conv_s, gated_s,
           pad0, pad1, sig_s, s0, s1, y0, y1, sems) = refs[:8], refs[8:]
    pads, s_s, y_s = (pad0, pad1), (s0, s1), (y0, y1)
    length, width = x_s.shape
    R = 256
    go = Mover(sems)
    x_c = go.start(x_in.at[idx[2]], x_s)
    w_c = go.pieces(in_copies(idx, own, held[:4], held[4:], w_s))
    sent = []
    for p in pads:
        p[0:8] = jnp.zeros((8, 3 * CH), f32)
    settle(x_c)
    for r in range(0, length, R):
        hat, _ = norm_parts(x_s[r : r + R].astype(f32))
        normed_s[r : r + R] = (hat * gain[...]).astype(bf16)
    settle(w_c)
    basis_c = go.start(basis_in, basis_s)

    def mix(i):
        w = jnp.concatenate([w_s[:, p * width + i * CH : p * width + (i + 1) * CH] for p in range(3)], 1)
        pads[i % 2][8:] = dot(normed_s[...], w)

    def smooth(i):
        pad = pads[i % 2]
        for r in range(0, length, R):
            now = []
            for p in range(3):
                c = blocks_of(p)
                g = slice(p * width + i * CH, p * width + (i + 1) * CH)
                m_s[p, r : r + R, blocks_of(i)] = pad[8 + r : 8 + r + R, c].astype(bf16)
                now.append(taps[0:1, g] * pad[8 + r : 8 + r + R, c] + taps[3:4, g] * pad[7 + r : 7 + r + R, c]
                           + taps[6:7, g] * pad[6 + r : 6 + r + R, c])
                qkv_s[p, r : r + R, blocks_of(i)] = now[p].astype(bf16)
            sig_s[r : r + R, blocks_of(i)] = (now[1] * now[2]).astype(bf16)
        sent.append(go.start(m_s.at[:, :, blocks_of(i)], m_o.at[:, :, blocks_of(i)]))
        sent.append(go.start(qkv_s.at[:, :, blocks_of(i)], qkv_o.at[:, :, blocks_of(i)]))

    def forth(i):
        s_s[i % 2][...] = dot(basis_s[...], sig_s[:, blocks_of(i)])

    def times(i):
        c = blocks_of(i)
        for r in range(0, length, R):
            at, lo = slice(r, r + R), slice(length + r, length + r + R)
            sc, ss = s_s[i % 2][at], s_s[i % 2][lo]
            sspec_s[at, c] = sc.astype(bf16)
            sspec_s[lo, c] = ss.astype(bf16)
            kc, ks = spec_s[at, c].astype(f32), spec_s[lo, c].astype(f32)
            y_s[i % 2][at] = (sc * kc - ss * ks).astype(bf16)
            y_s[i % 2][lo] = (sc * ks + ss * kc).astype(bf16)
        sent.append(go.start(sspec_s.at[:, c], sspec_o.at[:, c]))

    def back(i):
        c = blocks_of(i)
        conv = dot(back_s[...], y_s[i % 2][...])
        conv_s[:, c] = conv.astype(bf16)
        gated_s[:, c] = (qkv_s[0, :, c].astype(f32) * conv).astype(bf16)
        sent.append(go.start(conv_s.at[:, c], conv_o.at[:, c]))
        sent.append(go.start(gated_s.at[:, c], gated_o.at[:, c]))

    mix(0)
    mix(1)
    settle(basis_c)
    spec_c = go.start(spec_in, spec_s)
    smooth(0)
    forth(0)
    mix(2)
    settle(spec_c)
    back_c = go.start(back_in, back_s)
    sent.append(go.start(normed_s, normed_o))
    smooth(1)
    times(0)
    forth(1)
    settle(back_c)
    back(0)
    smooth(2)
    times(1)
    forth(2)
    back(1)
    times(2)
    back(2)
    settle(sent)


def mixer_front(idx, held, own_in, x, gain, taps, spec, basis, back):
    length, width = x.shape[1:]
    V = pltpu.VMEM
    low, three, tall = (length, width), (3, length, width), (2 * length, width)
    outs = [low, three, three, tall, low, low]
    return manual(
        front_kernel,
        13,
        (gain, taps),
        [sds(s, bf16) for s in outs],
        [ANY] * 6,
        [V(s, bf16) for s in (low, (width, 3 * width), tall, basis.shape, back.shape, *outs)]
        + [V((length + 8, 3 * CH), f32)] * 2 + [V(low, bf16)] + [V((2 * length, CH), f32)] * 2 + [V((2 * length, CH), bf16)] * 2,
        48,
        (idx, *held, own_in, x, spec, basis, back),
        6 * length * width * width + 8 * length * length * width,
        2 * (16 * length * width + 3 * width * width + 2 * basis.size),
    )


def gelu_parts(pre):
    cdf = 0.5 * (1.0 + lax.erf(pre * math.sqrt(0.5)))
    slope = cdf + pre * (jnp.exp(-0.5 * pre * pre) * (1.0 / math.sqrt(2.0 * math.pi)))
    return pre * cdf, slope


def live_rows(idx, rows, start=0):
    return (lax.broadcasted_iota(jnp.int32, (rows, 1), 0) + start < idx[3]).astype(f32)


def near_first(idx, ref, half):
    return (pl.ds(pl.multiple_of(idx[2] * half, 128), half), pl.ds(pl.multiple_of((1 - idx[2]) * half, 128), half))


def out_kernel(idx, *refs):
    rest, (own_out, x_ref, gated_ref, gain_ref, act0_ref, normed_ref, wo_ref, sem_o) = refs[:8], refs[8:]
    R, width = x_ref.shape
    start = pl.program_id(0) * R

    @pl.when(pl.program_id(0) == 0)
    def _():
        outs = out_copies(idx, own_out, rest[:4], rest[4:], wo_ref)
        start_all(outs, sem_o)
        wait_all(outs, sem_o)

    live = live_rows(idx, R, start)
    act0 = (live * (x_ref[...].astype(f32) + dot(gated_ref[...], wo_ref[...]))).astype(bf16)
    act0_ref[...] = act0
    hat, _ = norm_parts(act0.astype(f32))
    normed_ref[...] = (hat * gain_ref[...]).astype(bf16)


def mixer_out(idx, rest, own_out, x, gated, gain):
    length, width = gated.shape
    R = 512
    blk = rows_of(R, width)
    return call(
        out_kernel,
        (length // R,),
        [ANY] * 9 + [pl.BlockSpec((None, R, width), lambda i, idx: (idx[2], i, 0)), blk, whole(gain.shape)],
        [blk, blk],
        [sds((length, width), bf16)] * 2,
        [pltpu.VMEM((width, width), bf16), SEMS],
        (idx, *rest, own_out, x, gated, gain),
        2 * length * width * width,
        2 * (4 * length * width + width * width),
        prefetch=1,
    )


def up_kernel(idx, *refs):
    held, (own_up, og_ref, normed_ref, hidden_ref, slope_ref, near_ref, away_ref, wu_ref, turned, sem_u) = refs[:8], refs[8:]
    length, width = og_ref.shape
    half = width // 2
    c = pl.program_id(0)

    @pl.when(c == 0)
    def _():
        ups = up_copies(idx, own_up, held[:4], held[4:], wu_ref)
        start_all(ups, sem_u)
        live = live_rows(idx, length)
        for n, cols in enumerate(near_first(idx, og_ref, half)):
            turned[:, n * half : (n + 1) * half] = (live * og_ref[:, cols].astype(f32)).astype(bf16)
        wait_all(ups, sem_u)

    at = pl.ds(pl.multiple_of(c * width, width), width)
    hid, slope = gelu_parts(dot(normed_ref[...], wu_ref[:, at]))
    hid = hid.astype(bf16)
    hidden_ref[...] = hid
    slope_ref[...] = slope.astype(bf16)
    grad = dot(hid, turned[...], 0, 0).astype(bf16)
    near_ref[...] = grad[:, :half]
    away_ref[...] = grad[:, half:]


def mlp_up(idx, held, own_up, og, normed):
    length, width = normed.shape
    ff = own_up.shape[1]
    half = width // 2
    wide = cols_of(length, width)
    picked = pl.BlockSpec((None, length, width), lambda i, idx: (idx[2], 0, 0), pipeline_mode=pl.Buffered(1))
    return call(
        up_kernel,
        (ff // width,),
        [ANY] * 9 + [picked, whole((length, width))],
        [wide, wide, rows_of(width, half), rows_of(width, half)],
        [sds((length, ff), bf16), sds((length, ff), bf16), sds((ff, half), bf16), sds((ff, half), bf16)],
        [pltpu.VMEM((width, ff), bf16), pltpu.VMEM((length, width), bf16), SEMS],
        (idx, *held, own_up, og, normed),
        4 * length * width * ff,
        2 * (2 * length * width + 2 * width * ff + 2 * length * ff),
        prefetch=1,
    )


def down_kernel(idx, *refs):
    held, (own_up, own_down, og_ref, act0_ref, normed_ref, hidden_ref, slope_ref, gated_ref, gain_ref,
           act1_ref, ag_ref, branch_ref, gg_ref, near_ref, away_ref, near_out, away_out,
           wu_ref, wd_ref, acc, gn, branch, turned, sem_u, sem_d) = refs[:16], refs[16:]
    length, width = og_ref.shape
    half = width // 2
    c = pl.program_id(0)
    live = live_rows(idx, length)

    @pl.when(c == 0)
    def _():
        ups = up_copies(idx, own_up, held[:4], held[4:8], wu_ref)
        downs = down_copies(idx, own_down, held[8:12], held[12:], wd_ref)
        start_all(downs, sem_d)
        start_all(ups, sem_u)
        branch[...] = (live * og_ref[...].astype(f32)).astype(bf16)
        acc[...] = act0_ref[...].astype(f32)
        gn[...] = jnp.zeros((length, width), f32)
        wait_all(downs, sem_d)
        wait_all(ups, sem_u)

    at = pl.ds(pl.multiple_of(c * width, width), width)
    pre = (slope_ref[...].astype(f32) * dot(branch[...], wd_ref[at, :], 1, 1)).astype(bf16)
    for n, cols in enumerate(near_first(idx, turned, half)):
        turned[:, cols] = pre[:, n * half : (n + 1) * half]
    acc[...] += dot(hidden_ref[...], wd_ref[at, :])
    gn[...] += dot(pre, wu_ref[:, at], 1, 1)
    grad = dot(normed_ref[...], turned[...], 0, 0).astype(bf16)
    near_ref[...] = grad[:, :half]
    away_ref[...] = grad[:, half:]

    @pl.when(c == pl.num_programs(0) - 1)
    def _():
        act1_ref[...] = (live * acc[...]).astype(bf16)
        hat, inv = norm_parts(act0_ref[...].astype(f32))
        gg_ref[...] = jnp.sum(gn[...] * hat, axis=0, keepdims=True)
        ag = live * og_ref[...].astype(f32) + norm_back(gn[...], hat, inv, gain_ref[...])
        ag_ref[...] = ag
        branch_ref[...] = (live * ag).astype(bf16)
        for n, cols in enumerate(near_first(idx, branch_ref, half)):
            turned[:, n * half : (n + 1) * half] = branch_ref[:, cols]
        g_out = dot(gated_ref[...], turned[...], 0, 0).astype(bf16)
        near_out[...] = g_out[:, :half]
        away_out[...] = g_out[:, half:]


def mlp_down(idx, held_up, held_down, own_up, own_down, og, act0, normed, hidden, slope, gated, gain):
    length, width = act0.shape
    ff = own_up.shape[1]
    half = width // 2
    picked = pl.BlockSpec((None, length, width), lambda i, idx: (idx[2], 0, 0), pipeline_mode=pl.Buffered(1))
    one = whole((length, width))
    wide = cols_of(length, width)
    full = sds((length, width), bf16)
    col = pltpu.VMEM((length, width), f32)
    low = pltpu.VMEM((length, width), bf16)
    return call(
        down_kernel,
        (ff // width,),
        [ANY] * 18 + [picked, one, one, wide, wide, one, whole(gain.shape)],
        [one, one, one, whole((1, width)), cols_of(width, half), cols_of(width, half), whole((width, half)), whole((width, half))],
        [full, sds((length, width), f32), full, sds((1, width), f32), sds((width, ff // 2), bf16), sds((width, ff // 2), bf16),
         sds((width, half), bf16), sds((width, half), bf16)],
        [pltpu.VMEM((width, ff), bf16), pltpu.VMEM((ff, width), bf16), col, col, low, low, SEMS, SEMS],
        (idx, *held_up, *held_down, own_up, own_down, og, act0, normed, hidden, slope, gated, gain),
        8 * length * width * ff,
        2 * (8 * length * width + 3 * width * ff + 2 * length * ff),
        prefetch=1,
    )


def conv_back_kernel(idx, *refs):
    held, (own_out, branch_in, normed_in, m_in, qkv_in, conv_in, spec_in, sspec_in, basis_in, back_in, taps,
           g_o, near_o, away_o, gtaps_ref,
           w_s, branch_s, normed_s, m_s, qkv_s, conv_s, spec_s, sspec_s, basis_s, back_s,
           gpad0, gpad1, sig_s, s0, s1, y0, y1, both_s, gm0, gm1, g0_s, g1_s, kern0, kern1, near0, near1, away0, away1,
           sems) = refs[:8], refs[8:]
    gpads, s_s, y_s, gms, g_s, kerns, near_s, away_s = ((gpad0, gpad1), (s0, s1), (y0, y1), (gm0, gm1), (g0_s, g1_s),
                                                        (kern0, kern1), (near0, near1), (away0, away1))
    length, width = branch_s.shape
    half = width // 2
    hl = length // 2
    R = 256
    nb = width // CH
    go = Mover(sems)
    branch_c = go.start(branch_in, branch_s)
    w_c = go.pieces(out_copies(idx, own_out, held[:4], held[4:], w_s))
    basis_c = go.start(basis_in, basis_s)

    def fetch(i):
        c = blocks_of(i)
        return [go.start(qkv_in.at[:, :, c], qkv_s.at[:, :, c]), go.start(conv_in.at[:, c], conv_s.at[:, c])]

    def fetch_spectra(i):
        c = blocks_of(i)
        return [go.start(spec_in.at[:, c], spec_s.at[:, c]), go.start(sspec_in.at[:, c], sspec_s.at[:, c])]

    def fetch_mixed(i):
        c = blocks_of(i)
        return go.start(m_in.at[:, :, c], m_s.at[:, :, c])

    for p in gpads:
        p[length : length + 8] = jnp.zeros((8, 3 * CH), f32)
    sent = [[], []]
    settle(branch_c, w_c)
    first_c = fetch(0)

    def spread_back(i):
        s_s[i % 2][0:length] = dot(branch_s[...], w_s[blocks_of(i), :], 1, 1)

    def gate(i):
        c = blocks_of(i)
        for r in range(0, length, R):
            at = slice(r, r + R)
            gg = s_s[i % 2][at]
            sig_s[at, c] = (gg * qkv_s[0, at, c].astype(f32)).astype(bf16)
            gpads[i % 2][at, 0:CH] = gg * conv_s[at, c].astype(f32)

    def forth(i):
        s_s[i % 2][...] = dot(basis_s[...], sig_s[:, blocks_of(i)])

    def times(i):
        c = blocks_of(i)
        y = y_s[i % 2]
        for r in range(0, length, R):
            at, lo = slice(r, r + R), slice(length + r, length + r + R)
            gc, gs = s_s[i % 2][at], s_s[i % 2][lo]
            kc, ks = spec_s[at, c].astype(f32), spec_s[lo, c].astype(f32)
            y[at, 0:CH] = (kc * gc + ks * gs).astype(bf16)
            y[lo, 0:CH] = (kc * gs - ks * gc).astype(bf16)
            sc, ss = sspec_s[at, c].astype(f32), sspec_s[lo, c].astype(f32)
            y[at, CH:] = (sc * gc + ss * gs).astype(bf16)
            y[lo, CH:] = (sc * gs - ss * gc).astype(bf16)

    def back(i):
        both_s[...] = dot(back_s[...], y_s[i % 2][...])

    def unsmooth(i):
        b = blocks_of(i)
        gpad, gm, kern = gpads[i % 2], gms[i % 2], kerns[i % 2]
        settle(sent[i % 2])
        for r in range(0, length, R):
            at = slice(r, r + R)
            g_sig = both_s[at, :CH]
            gpad[at, CH : 2 * CH] = g_sig * qkv_s[2, at, b].astype(f32)
            gpad[at, 2 * CH :] = g_sig * qkv_s[1, at, b].astype(f32)
            position = (lax.broadcasted_iota(jnp.int32, (R, 1), 0) + r).astype(f32)
            kern[:, at] = (both_s[at, CH:] * (jnp.exp(-decay_rate * position) / length)).T.astype(bf16)
        sums = [[jnp.zeros((1, CH), f32)] * 3 for _ in range(3)]
        for r in range(0, length, R):
            at = slice(r, r + R)
            for p in range(3):
                c = blocks_of(p)
                t = slice(p * width + i * CH, p * width + (i + 1) * CH)
                now = [gpad[r + n : r + n + R, c] for n in range(3)]
                g = (taps[0:1, t] * now[0] + taps[3:4, t] * now[1] + taps[6:7, t] * now[2]).astype(bf16)
                g_s[i % 2][p, at] = g
                for n in range(2):
                    to = jnp.where(idx[2] == n, 0, half) + p * (CH // 2)
                    gm[at, pl.ds(pl.multiple_of(to, 128), CH // 2)] = g[:, n * (CH // 2) : (n + 1) * (CH // 2)]
                mixed = m_s[p, at, b].astype(f32)
                sums[p] = [sums[p][n] + jnp.sum(now[n] * mixed, axis=0, keepdims=True) for n in range(3)]
        for p in range(3):
            for n in range(3):
                gtaps_ref[3 * p + n : 3 * p + n + 1, b] = sums[p][n]
        side = slice(3 * half, 3 * half + hl)
        mine, other = near_first(idx, kern, hl)
        sent[i % 2] = [go.start(g_s[i % 2], g_o.at[:, :, b]), go.start(kern.at[:, mine], near_o.at[b, side]),
                       go.start(kern.at[:, other], away_o.at[b, side])]

    def grad(i):
        g = dot(normed_s[...], gms[i % 2][...], 0, 0).astype(bf16)
        near_s[i % 2][...] = g[:, :half]
        away_s[i % 2][...] = g[:, half:]
        c = slice(i * half, (i + 1) * half)
        sent[i % 2] += [go.start(near_s[i % 2], near_o.at[:, c]), go.start(away_s[i % 2], away_o.at[:, c])]

    spread_back(0)
    spread_back(1)
    settle(basis_c, first_c)
    spectra_c = fetch_spectra(0)
    gate(0)
    forth(0)
    settle(spectra_c)
    back_c = go.start(back_in, back_s)
    next_c = fetch(1)
    times(0)
    settle(next_c, back_c)
    spectra_c = fetch_spectra(1)
    mixed_c = fetch_mixed(0)
    normed_c = go.start(normed_in, normed_s)
    back(0)
    gate(1)
    forth(1)
    spread_back(2)
    settle(spectra_c, mixed_c, normed_c)
    next_c = fetch(2)
    mixed_c = fetch_mixed(1)
    spectra_c = fetch_spectra(2)
    unsmooth(0)
    times(1)
    back(1)
    grad(0)
    settle(next_c, mixed_c, spectra_c)
    mixed_c = fetch_mixed(2)
    gate(2)
    forth(2)
    unsmooth(1)
    times(2)
    grad(1)
    back(2)
    settle(mixed_c)
    unsmooth(2)
    grad(2)
    settle(sent)


def conv_backward(idx, held, own_out, branch, normed, mixed, qkv, taps, conv, spec, sspec, basis, back):
    length, width = branch.shape
    half = width // 2
    mix = (width, 3 * half + length // 2)
    V = pltpu.VMEM
    low, three, tall = (length, width), (3, length, width), (2 * length, width)
    twice = lambda s, t: [V(s, t)] * 2
    return manual(
        conv_back_kernel,
        18,
        (taps,),
        [sds(three, bf16), sds(mix, bf16), sds(mix, bf16), sds((9, width), f32)],
        [ANY] * 3 + [whole((9, width))],
        [V(s, bf16) for s in ((width, width), low, low, three, three, low, tall, tall, basis.shape, back.shape)]
        + twice((length + 8, 3 * CH), f32) + [V(low, bf16)] + twice((2 * length, CH), f32) + twice((2 * length, 2 * CH), bf16)
        + [V((length, 2 * CH), f32)] + twice((length, 3 * CH), bf16) + twice((3, length, CH), bf16) + twice((CH, length), bf16)
        + twice((width, half), bf16) + twice((width, half), bf16),
        64,
        (idx, *held, own_out, branch, normed, mixed, qkv, conv, spec, sspec, basis, back),
        8 * length * width * width + 12 * length * length * width,
        2 * (22 * length * width + 2 * basis.size + 2 * mix[0] * mix[1]),
    )


def norm_back_kernel(idx, *refs):
    held, (own_ref, g_ref, x_ref, masked_ref, gain_ref, ag_ref, gg_ref, wi_ref, sems) = refs[:8], refs[8:]
    width = x_ref.shape[1]

    @pl.when(pl.program_id(0) == 0)
    def _():
        copies = in_copies(idx, own_ref, held[:4], held[4:], wi_ref)
        start_all(copies, sems)
        wait_all(copies, sems)

    gn = dot(jnp.concatenate([g_ref[p] for p in range(3)], 1), wi_ref[...], 1, 1)
    hat, inv = norm_parts(x_ref[...].astype(f32))
    part = jnp.sum(gn * hat, axis=0, keepdims=True)

    @pl.when(pl.program_id(0) == 0)
    def _():
        gg_ref[...] = part

    @pl.when(pl.program_id(0) > 0)
    def _():
        gg_ref[...] += part

    ag_ref[...] = masked_ref[...].astype(f32) + norm_back(gn, hat, inv, gain_ref[...])


def input_backward(idx, held, own_in, g_mixed, x, masked, gain):
    length, width = masked.shape
    R = 512
    blk = rows_of(R, width)
    return call(
        norm_back_kernel,
        (length // R,),
        [ANY] * 9 + [pl.BlockSpec((3, R, width), lambda i, *_: (0, i, 0)),
                     pl.BlockSpec((None, R, width), lambda i, idx: (idx[2], i, 0)), blk, whole(gain.shape)],
        [blk, pl.BlockSpec((1, width), lambda *_: (0, 0))],
        [sds((length, width), f32), sds((1, width), f32)],
        [pltpu.VMEM((width, 3 * width), bf16), SEMS],
        (idx, *held, own_in, g_mixed, x, masked, gain),
        6 * length * width * width,
        2 * (7 * length * width + 3 * width * width),
        prefetch=1,
    )


def unpack_mlp_kernel(idx, all_ref, up, down, out):
    part = up.shape[0]
    q = up.shape[1] // 4
    h = down.shape[1] // 2
    r = part // 4
    for n in range(8):
        d, side = n // 2, n % 2
        cols = slice(side * h, side * h + h)
        down[d * part : (d + 1) * part, cols] = all_ref[n, 0:part].astype(f32)
        up[:, d * q + side * h : d * q + side * h + h] = all_ref[n, part : 2 * part].astype(f32)
        out[d * r : (d + 1) * r, cols] = all_ref[n, 2 * part :].astype(f32)


def unpack_mix_kernel(idx, *refs):
    held, (g_in, g_kern) = refs[:8], refs[8:]
    part, length = g_kern.shape
    width = 4 * part
    r = part // 4
    h = width // 2
    b = CH // 2
    for e in range(4):
        at = pl.ds(pl.multiple_of((idx[1] ^ e) * r, 16), r)
        for ref, side in ((held[e], idx[2]), (held[4 + e], 1 - idx[2])):
            for i in range(width // CH):
                for p in range(3):
                    c = i * h + p * b
                    g_in[at, pl.ds(pl.multiple_of(p * width + i * CH + side * b, 128), b)] = ref[:, c : c + b].astype(f32)
            g_kern[at, pl.ds(pl.multiple_of(side * (length // 2), 128), length // 2)] = ref[:, 3 * h :].astype(f32)


def unpack(kernel, idx, held, shapes):
    return call(
        kernel,
        (1,),
        [whole(h.shape) for h in held],
        [whole(s) for s in shapes],
        [sds(s, f32) for s in shapes],
        [],
        (idx, *held),
        0,
        sum(6 * math.prod(s) for s in shapes),
        prefetch=1,
    )


SWAP = [(0, 1), (1, 0)]


def shift(k):
    return [(i, (i + k) % 4) for i in range(4)]


def flip(e):
    return [(i, i ^ e) for i in range(4)]


def tie(value, *others):
    return lax.optimization_barrier((value, *others))[0]


def over_line(piece):
    return jnp.concatenate([lax.ppermute(piece, "chan", shift(k)) for k in SHIFTS], 0)


def over_plane(near):
    return [near] + [lax.ppermute(near, "dp", flip(e)) for e in (1, 2, 3)]


def over_chip(mine):
    return mine + [lax.ppermute(m, "section", SWAP) for m in mine]


def total(parts):
    out = parts[0].astype(f32)
    for p in parts[1:]:
        out += p.astype(f32)
    return out.astype(bf16)


def fold_plane(parts):
    return total([parts[0]] + [lax.ppermute(parts[e], "dp", flip(e)) for e in (1, 2, 3)])


def fold_line(held, z):
    def at(k):
        return lax.dynamic_index_in_dim(held, (z + k) % 4, 0, keepdims=False)

    return total([at(0)] + [lax.ppermute(at(k), "chan", shift(k)) for k in SHIFTS])


def cut(v, at, size, axis):
    return lax.dynamic_slice_in_dim(v, at, size, axis)


def fast_body(inputs, lengths, out_grad, ln_mix_gain, w_in, short_taps, long_taps, w_out, ln_mlp_gain, w_up, w_down):
    z, d, s = lax.axis_index("chan"), lax.axis_index("dp"), lax.axis_index("section")
    length = inputs.shape[2]
    width = inputs.shape[3]
    part = w_in.shape[1]
    ff = w_up.shape[2]
    half = width // 2
    hl = length // 2
    r = part // 4
    count = lax.dynamic_index_in_dim(lengths[:, 0], s, 0, keepdims=False)
    idx = jnp.stack([z, d, s, count]).astype(jnp.int32)
    x, og = inputs[:, 0], out_grad[:, 0]
    table = odd_basis(length)
    basis, back = jnp.asarray(table), jnp.asarray(np.ascontiguousarray(table.T))
    first = s == 0

    def after(parts, values):
        return lax.optimization_barrier((list(parts), list(values)))

    def both_cores(near, away):
        return total([near, lax.ppermute(away, "section", SWAP)])

    def stacked(own_first, own_second, other, dtype):
        keep = jnp.where(first, own_first, own_second).astype(dtype)
        other = other.astype(dtype)
        both = jnp.stack([jnp.where(first, keep, other), jnp.where(first, other, keep)])
        return both[None, :, None]

    def to_plane(parts):
        return [parts[0]] + [lax.ppermute(parts[e], "dp", flip(e)) for e in (1, 2, 3)]

    def line_sum(held):
        return lax.psum_scatter(held, "chan", scatter_dimension=0, tiled=False)

    own_in, own_out, own_up, own_down = w_in[0], w_out[0], w_up[0], w_down[0]
    own_taps = long_taps[0].T
    small = jnp.concatenate([ln_mix_gain, ln_mlp_gain, short_taps[0].reshape(9, part)], 0)
    own_small = jnp.pad(small.T, ((0, 0), (0, 128 - 11)))
    piece = jnp.concatenate([cut(own_taps, s * hl, hl, 1), own_small], 1)
    split = piece.shape[1]
    piece = jnp.concatenate([cut(piece, d * r, r, 0), cut(cut(own_in, d * r, r, 0), s * 3 * half, 3 * half, 1)], 1)
    near = over_line(piece)
    near_rest, near_in = near[:, :split], near[:, split:]
    plane_rest = over_plane(near_rest)
    plane_in = over_plane(near_in)
    piece_mlp = jnp.concatenate(
        [
            cut(cut(own_down, d * part, part, 0), s * half, half, 1),
            cut(own_up, s * (ff // 2) + d * (ff // 8), ff // 8, 1),
            cut(cut(own_out, d * r, r, 0), s * half, half, 1),
        ],
        0,
    )
    line_mlp = lax.all_gather(tie(piece_mlp, near), "chan", axis=0)
    held_rest = over_chip(plane_rest)

    plane_in, (spec, small, taps) = after(
        plane_in, kernel_spectra(idx, held_rest, tie(own_taps, near_in), own_small, basis)
    )
    held_in = over_chip(plane_in)
    gain_mix, gain_mlp = small[0:1], small[1:2]
    line_mlp = [lax.dynamic_index_in_dim(line_mlp, (z + 4 - k) % 4, 0, keepdims=False) for k in SHIFTS]
    near_up = jnp.concatenate([v[part:] for v in line_mlp], 0)
    near_down = jnp.concatenate([v[:part] for v in line_mlp], 0)
    plane_up = over_plane(near_up)
    plane_down = over_plane(near_down)
    plane_up, (normed0, mixed, qkv, sspec, conv, gated) = after(
        plane_up, mixer_front(idx, held_in, own_in, x, gain_mix, taps, tie(spec, near_up, near_down), basis, back)
    )
    held_up = over_chip(plane_up)
    act0, normed1 = mixer_out(idx, held_up, own_out, x, gated, gain_mlp)
    plane_down, (hidden, slope, near, away) = after(plane_down, mlp_up(idx, held_up, own_up, og, normed1))
    held_down = over_chip(plane_down)

    h_down = both_cores(near, away).reshape(4, 4, part, half)
    sent_down = [lax.dynamic_index_in_dim(h_down, d ^ e, 1, keepdims=False) for e in range(4)]
    got_down = to_plane(sent_down)
    got_down, (act1, ag1, branch0, g_gain_mlp, near, away, near_out, away_out) = after(
        got_down,
        mlp_down(
            idx, held_up, held_down, own_up, own_down, og, act0, normed1, hidden, tie(slope, *sent_down), gated, gain_mlp
        ),
    )
    h_up = both_cores(near, away).reshape(4, part, ff // 2)
    h_out = both_cores(near_out, away_out).reshape(4, 4, r, half)
    sent_up = [
        jnp.concatenate([cut(h_up, (d ^ e) * half, half, 2), lax.dynamic_index_in_dim(h_out, d ^ e, 1, keepdims=False)], 1)
        for e in range(4)
    ]
    got_up = to_plane(sent_up)

    branch_late = tie(branch0, *sent_up)
    got_up, (g_mixed, near, away, g_taps) = after(
        got_up,
        conv_backward(idx, held_up, own_out, branch_late, normed0, mixed, qkv, taps, conv, spec, sspec, basis, back),
    )
    u_mlp = jnp.concatenate([total(got_down), total(got_up)], 1)
    p_mlp = line_sum(u_mlp)
    h_mix = both_cores(near, away).reshape(4, 4, r, 3 * half + hl)
    sent_mix = [lax.dynamic_index_in_dim(h_mix, d ^ e, 1, keepdims=False) for e in range(4)]
    got_mix = to_plane(sent_mix)
    ag0, g_gain_mix = input_backward(idx, held_in, own_in, tie(g_mixed, u_mlp, *sent_mix), x, branch0, gain_mix)
    tiny = jnp.concatenate([g_gain_mix, g_gain_mlp, g_taps], 0)
    tiny += lax.ppermute(tiny, "section", SWAP)
    (*got_mix, p_mlp), (ag0, tiny) = after([*got_mix, p_mlp], [ag0, tiny])
    all_mlp = lax.all_gather(p_mlp, ("dp", "section"), axis=0)
    u_mix = total(got_mix)
    sent_line = [lax.dynamic_index_in_dim(u_mix, (z + k) % 4, 0, keepdims=False) for k in (0, *SHIFTS)]
    got_line = [sent_line[0]] + [lax.ppermute(v, "chan", shift(k)) for k, v in zip(SHIFTS, sent_line[1:])]
    tiny = tie(tiny, *sent_line)
    tiny += lax.ppermute(tiny, "dp", flip(1))
    ag0_late = tie(ag0, *sent_line)
    swapped = jnp.concatenate([jnp.where(first, act1, act0), jnp.where(first, ag1, ag0_late).astype(bf16)], 0)
    swapped = lax.ppermute(swapped, "section", SWAP)
    out_act = stacked(act0, act1, swapped[:length], bf16)
    out_ag = stacked(ag0_late, ag1, swapped[length:], f32)
    got_line, (tiny, out_act, out_ag) = after(got_line, [tiny, out_act, out_ag])
    g_up, g_down, g_out = unpack(unpack_mlp_kernel, idx, [all_mlp], [(part, ff), (4 * part, width), (part, width)])
    p_mix = total(got_line)
    plane_mix = over_plane(p_mix)
    tiny = tie(tiny, p_mix)
    tiny += lax.ppermute(tiny, "dp", flip(2))
    plane_mix, (tiny,) = after(plane_mix, [tiny])
    got_tiny = [lax.ppermute(tiny, "chan", flip(e)) for e in (1, 2, 3)]
    held_mix, (g_up, g_down, g_out) = after(over_chip(plane_mix), [g_up, g_down, g_out])
    g_in, g_kern = unpack(unpack_mix_kernel, idx, held_mix, [(part, 3 * width), (part, length)])
    got_tiny, (g_in, g_kern) = after(got_tiny, [g_in, g_kern])
    tiny = (tiny + got_tiny[0]) + (got_tiny[1] + got_tiny[2])

    mine = cut(tiny[0:2], z * part, part, 1)
    g_taps = tiny[2:11].reshape(3, 3, width).transpose(1, 0, 2).reshape(3, 3 * width)
    g_taps = cut(g_taps, z * 3 * part, 3 * part, 1)

    return (
        out_act,
        out_ag,
        mine[0:1],
        g_in[None],
        g_taps[None],
        g_kern.T[None],
        g_out[None],
        mine[1:2],
        g_up[None],
        g_down[None],
    )


def fits(mesh):
    return mesh.shape["chan"] == 4 and mesh.shape["dp"] == 4 and mesh.shape["section"] == 2


def shift_down(v, n):
    return jnp.pad(v, ((n, 0), (0, 0)))[: v.shape[0]]


def shift_up(v, n):
    return jnp.pad(v, ((0, n), (0, 0)))[n:]


def plain_body(inputs, lengths, out_grad, ln_mix_gain, w_in, short_taps, long_taps, w_out, ln_mlp_gain, w_up, w_down):
    own = lax.axis_index("section")
    length, width = inputs.shape[2:]
    position = lax.broadcasted_iota(jnp.int32, (length, 1), 0)
    x = lax.dynamic_index_in_dim(inputs[:, 0], own, 0, keepdims=False).astype(f32)
    og = lax.dynamic_index_in_dim(out_grad[:, 0], own, 0, keepdims=False)
    live = (position < lax.dynamic_index_in_dim(lengths[:, 0], own, 0, keepdims=False)).astype(f32)

    def rows(w):
        return lax.all_gather(w[0], "chan", axis=0, tiled=True)

    def cols(w):
        return lax.all_gather(w[0], "chan", axis=1, tiled=True)

    gain_mix = cols(ln_mix_gain[None])[0].astype(f32)
    gain_mlp = cols(ln_mlp_gain[None])[0].astype(f32)
    taps = cols(short_taps).astype(f32)
    kern = cols(long_taps).astype(f32)
    proj_in, proj_out, proj_up, proj_down = rows(w_in), rows(w_out), rows(w_up), rows(w_down)

    basis = jnp.asarray(odd_basis(length))
    decay = jnp.exp(-decay_rate * position.astype(f32))
    half = length

    def spectrum(v):
        both = dot(basis, v)
        return both[:half], both[half:]

    def back(cos_part, sin_part):
        return dot(basis, jnp.concatenate([cos_part, sin_part], 0).astype(bf16), 0, 0)

    kc, ks = spectrum((kern * decay).astype(bf16))
    kc, ks = kc / length, ks / length
    hat0, inv0 = norm_parts(x)
    normed0 = (hat0 * gain_mix).astype(bf16)
    mixed = dot(normed0, proj_in)
    smooth = taps[0] * mixed + taps[1] * shift_down(mixed, 1) + taps[2] * shift_down(mixed, 2)
    query, key, value = smooth[:, :width], smooth[:, width : 2 * width], smooth[:, 2 * width :]
    sc, ss = spectrum((key * value).astype(bf16))
    conv = back(sc * kc - ss * ks, sc * ks + ss * kc)
    gated = (query * conv).astype(bf16)
    act0 = (live * (x + dot(gated, proj_out))).astype(bf16)
    x1 = act0.astype(f32)
    hat1, inv1 = norm_parts(x1)
    normed1 = (hat1 * gain_mlp).astype(bf16)
    pre = dot(normed1, proj_up)
    cdf = 0.5 * (1.0 + lax.erf(pre * math.sqrt(0.5)))
    hidden = (pre * cdf).astype(bf16)
    act1 = (live * (x1 + dot(hidden, proj_down))).astype(bf16)
    masked1 = live * og.astype(f32)
    branch1 = masked1.astype(bf16)
    g_down = dot(hidden, branch1, 0, 0)
    slope = cdf + pre * (jnp.exp(-0.5 * pre * pre) * (1.0 / math.sqrt(2.0 * math.pi)))
    pre_grad = (slope * dot(branch1, proj_down, 1, 1)).astype(bf16)
    g_up = dot(normed1, pre_grad, 0, 0)
    gn1 = dot(pre_grad, proj_up, 1, 1)
    g_gain_mlp = jnp.sum(gn1 * hat1, axis=0)
    ag1 = masked1 + norm_back(gn1, hat1, inv1, gain_mlp)
    ag1_low = ag1.astype(bf16)
    masked0 = live * ag1_low.astype(f32)
    branch0 = masked0.astype(bf16)
    g_out = dot(gated, branch0, 0, 0)
    grad_gated = dot(branch0, proj_out, 1, 1)
    gc, gs = spectrum((grad_gated * query).astype(bf16))
    g_kern = back(sc * gc + ss * gs, sc * gs - ss * gc) * (decay / length)
    g_sig = back(kc * gc + ks * gs, kc * gs - ks * gc)
    g_smooth = jnp.concatenate([grad_gated * conv, g_sig * value, g_sig * key], 1)
    g_taps = jnp.stack([jnp.sum(g_smooth * shift_down(mixed, n), axis=0) if n else jnp.sum(g_smooth * mixed, axis=0) for n in range(3)])
    g_mixed = (taps[0] * g_smooth + taps[1] * shift_up(g_smooth, 1) + taps[2] * shift_up(g_smooth, 2)).astype(bf16)
    g_in = dot(normed0, g_mixed, 0, 0)
    gn0 = dot(g_mixed, proj_in, 1, 1)
    g_gain_mix = jnp.sum(gn0 * hat0, axis=0)
    ag0 = masked0 + norm_back(gn0, hat0, inv0, gain_mix)

    swap = [(0, 1), (1, 0)]
    first = own == 0

    def exchange(own_first, own_second, dtype):
        keep = jnp.where(first, own_first, own_second).astype(dtype)
        other = lax.ppermute(jnp.where(first, own_second, own_first).astype(bf16), "section", swap).astype(dtype)
        both = jnp.stack([jnp.where(first, keep, other), jnp.where(first, other, keep)])
        return both[None, :, None]

    def reduced(g, dim):
        part = lax.psum_scatter(g.astype(bf16), "chan", scatter_dimension=dim, tiled=True)
        return lax.psum(part, ("section", "dp")).astype(f32)[None]

    return (
        exchange(act0, act1, bf16),
        exchange(ag0, ag1, f32),
        reduced(g_gain_mix, 0),
        reduced(g_in, 0),
        reduced(g_taps, 1),
        reduced(g_kern, 1),
        reduced(g_out, 0),
        reduced(g_gain_mlp, 0),
        reduced(g_up, 0),
        reduced(g_down, 0),
    )


def solution(mesh):
    return jax.shard_map(
        fast_body if fits(mesh) else plain_body,
        mesh=mesh,
        in_specs=(
            P(None, ("dp", "chan"), None, None),
            P(None, ("dp", "chan")),
            P(None, ("dp", "chan"), None, None),
            P(None, "chan"),
            P(None, "chan", None),
            P(None, None, "chan"),
            P(None, None, "chan"),
            P(None, "chan", None),
            P(None, "chan"),
            P(None, "chan", None),
            P(None, "chan", None),
        ),
        out_specs=(
            P("section", None, ("dp", "chan"), None, None),
            P("section", None, ("dp", "chan"), None, None),
            P(None, "chan"),
            P(None, "chan", None),
            P(None, None, "chan"),
            P(None, None, "chan"),
            P(None, "chan", None),
            P(None, "chan"),
            P(None, "chan", None),
            P(None, "chan", None),
        ),
        check_vma=False,
    )
```

profile of v0, /device:TPU:0, one launch (start us, length us, event | category | flops | bytes accessed | tf_op | source)
XLA Modules:
  0.0 338.0 jit_solution(11543467409352219338)
XLA Ops:
  10.9 3.1 collective-permute-start
  23.5 7.9 %collective-permute-done.2 = bf16[48,1792]{1,0:T(8,128)(2,1)S(1)} collective-permute-done((bf16[48,1792]{1,0:T(8,128)(2,1)S(1)}, bf16[48,1792]{1,0:T(8,128)(2,1)S(1)}, u32[]{:S(2)}, u32[]{:S(2)}) %collective-permute-start.2) | collective-permute-done | bytes 172064 | tf_op jit(solution)/shard_map/ppermute | solution.py:798
  35.1 4.0 %collective-permute-done.12.refs_1_ = bf16[144,640]{1,0:T(8,128)(2,1)S(1)} collective-permute-done((bf16[144,640]{1,0:T(8,128)(2,1)S(1)}, bf16[144,640]{1,0:T(8,128)(2,1)S(1)}, u32[]{:S(2)}, u32[]{:S(2)}) %collective-permute-start.12) | collective-permute-done | bytes 184352 | tf_op jit(solution)/shard_map/ppermute | solution.py:802
  39.2 4.2 %collective-permute-done.13.refs_2_ = bf16[144,640]{1,0:T(8,128)(2,1)S(1)} collective-permute-done((bf16[144,640]{1,0:T(8,128)(2,1)S(1)}, bf16[144,640]{1,0:T(8,128)(2,1)S(1)}, u32[]{:S(2)}, u32[]{:S(2)}) %collective-permute-start.13) | collective-permute-done | bytes 184352 | tf_op jit(solution)/shard_map/ppermute | solution.py:802
  50.7 10.6 %shard_map.204 = (bf16[2048,768]{1,0:T(8,128)(2,1)}, f32[8,768]{1,0:T(8,128)}, f32[8,2304]{1,0:T(8,128)}) custom-call(s32[4]{0:T(128)} %pad_add_fusion.idx, bf16[144,640]{1,0:T(8,128)(2,1)} %copy-done.29, bf16[144,640]{1,0:T(8,128)(2,1)} %copy-done.48, bf16[144,640]{1,0:T(8,128)(2,1)} %copy-done.49, bf16[144,640]{1,0:T(8,128)(2,1)} %copy-done.50, ...), custom_call_target="tpu_custom_call" | custom-call | flops 3221225472 | bytes 8912896 | tf_op jit(solution)/shard_map/pallas_call | solution.py:48
  71.9 22.9 %shard_map.205 = (bf16[1024,768]{1,0:T(8,128)(2,1)}, bf16[3,1024,768]{2,1,0:T(8,128)(2,1)}, bf16[3,1024,768]{2,1,0:T(8,128)(2,1)}, bf16[2048,768]{1,0:T(8,128)(2...) custom-call(s32[4]{0:T(128)} %pad_add_fusion.idx, bf16[144,1152]{1,0:T(8,128)(2,1)} %copy-done.26, ...), custom_call_target="tpu_custom_call" | custom-call | flops 10066329600 | bytes 37093376 | tf_op jit(solution)/shard_map/pallas_call | solution.py:48
  101.2 7.1 %shard_map.206 = (bf16[1024,768]{1,0:T(8,128)(2,1)}, bf16[1024,768]{1,0:T(8,128)(2,1)}) custom-call(s32[4]{0:T(128)} %pad_add_fusion.idx, bf16[720,384]{1,0:T(8,128)(2,1)} %copy-done.10, bf16[720,384]{1,0:T(8,128)(2,1)} %copy-done.18, bf16[720,384]{1,0:T(8,128)(2,1)} %copy-done.19, bf16[720,384]{1,0:T(8,128)(2,1)} %copy-done.20, ...), custom_call_target="tpu_custom_call" | custom-call | flops 1207959552 | bytes 7471104 | tf_op jit(solution)/shard_map/pallas_call | solution.py:48
  108.3 20.0 %shard_map.207 = (bf16[1024,3072]{1,0:T(8,128)(2,1)}, bf16[1024,3072]{1,0:T(8,128)(2,1)}, bf16[3072,384]{1,0:T(8,128)(2,1)}, bf16[3072,384]{1,0:T(8,128)(2,1)}) custom-call(s32[4]{0:T(128)} %pad_add_fusion.idx, bf16[720,384]{1,0:T(8,128)(2,1)} %copy-done.10, bf16[720,384]{1,0:T(8,128)(2,1)} %copy-done.18, bf16[720,384]{1,0:T(8,128)(2,1)} %copy-done.19, ...), custom_call_target="tpu_custom_call" | custom-call | flops 9663676416 | bytes 25165824 | tf_op jit(solution)/shard_map/pallas_call | solution.py:48
  130.4 5.6 %collective-permute-done.27 = bf16[3072,384]{1,0:T(8,128)(2,1)S(1)} collective-permute-done((bf16[3072,384]{1,0:T(8,128)(2,1)}, bf16[3072,384]{1,0:T(8,128)(2,1)S(1)}, u32[]{:S(2)}, u32[]{:S(2)}) %collective-permute-start.27) | collective-permute-done | bytes 2359328 | tf_op jit(solution)/shard_map/ppermute | solution.py:851
  142.2 38.3 %shard_map.208 = (bf16[1024,768]{1,0:T(8,128)(2,1)}, f32[1024,768]{1,0:T(8,128)}, bf16[1024,768]{1,0:T(8,128)(2,1)}, f32[1,768]{1,0:T(1,128)}, bf16[768,1536]{1,...) custom-call(s32[4]{0:T(128)} %pad_add_fusion.idx, ...), custom_call_target="tpu_custom_call" | custom-call | flops 19327352832 | bytes 39321600 | tf_op jit(solution)/shard_map/pallas_call | solution.py:48
  181.8 5.1 %collective-permute-done.36 = bf16[768,384]{1,0:T(8,128)(2,1)S(1)} collective-permute-done((bf16[768,384]{1,0:T(8,128)(2,1)}, bf16[768,384]{1,0:T(8,128)(2,1)S(1)}, u32[]{:S(2)}, u32[]{:S(2)}) %collective-permute-start.36) | collective-permute-done | bytes 589856 | tf_op jit(solution)/shard_map/ppermute | solution.py:851
  188.3 2.4 add_convert_fusion.1
  197.4 37.0 %shard_map.209 = (bf16[3,1024,768]{2,1,0:T(8,128)(2,1)}, bf16[768,1664]{1,0:T(8,128)(2,1)}, bf16[768,1664]{1,0:T(8,128)(2,1)}, f32[9,768]{1,0:T(8,128)}) custom-call(s32[4]{0:T(128)} %pad_add_fusion.idx, bf16[720,384]{1,0:T(8,128)(2,1)} %copy-done.10, bf16[720,384]{1,0:T(8,128)(2,1)} %copy-done.18, bf16[720,384]{1,0:T(8,128)(2,1)} %copy-done.19, ...), custom_call_target="tpu_custom_call" | custom-call | flops 14495514624 | bytes 48103424 | tf_op jit(solution)/shard_map/pallas_call | solution.py:48
  239.6 2.4 add_convert_fusion
  247.0 12.4 %shard_map.210 = (f32[1024,768]{1,0:T(8,128)}, f32[1,768]{1,0:T(1,128)}) custom-call(s32[4]{0:T(128)} %pad_add_fusion.idx, bf16[144,1152]{1,0:T(8,128)(2,1)} %copy-done.26, bf16[144,1152]{1,0:T(8,128)(2,1)} %copy-done.46, bf16[144,1152]{1,0:T(8,128)(2,1)} %copy-done.44, bf16[144,1152]{1,0:T(8,128)(2,1)} %copy-done.45, bf16[144,1152]{1,0:T(8,128)(2,1)} %copy-done.47, ...), custom_call_target="tpu_custom_call" | custom-call | flops 3623878656 | bytes 14548992 | tf_op jit(solution)/shard_map/pallas_call | solution.py:48
  261.7 5.6 %reduce-scatter.2.cloned.1.call-done = bf16[1,432,384]{2,1,0:T(8,128)(2,1)} async-done(((bf16[4,432,384]{2,1,0:T(8,128)(2,1)}), bf16[1,432,384]{2,1,0:T(8,128)(2,1)}) %reduce-scatter.2.cloned.1.call-update) | async-done | bytes 331792 | tf_op jit(solution)/shard_map/reduce_scatter | solution.py:863
  267.2 6.4 %collective-permute-done.42 = bf16[4,48,1664]{2,1,0:T(8,128)(2,1)} collective-permute-done((bf16[4,48,1664]{2,1,0:T(8,128)(2,1)}, bf16[4,48,1664]{2,1,0:T(8,128)(2,1)}, u32[]{:S(2)}, u32[]{:S(2)}) %collective-permute-start.42) | collective-permute-done | bytes 639008 | tf_op jit(solution)/shard_map/ppermute | solution.py:860
  282.3 4.1 %collective-permute-start.46 = (bf16[48,1664]{1,0:T(8,128)(2,1)}, bf16[48,1664]{1,0:T(8,128)(2,1)S(1)}, u32[]{:S(2)}, u32[]{:S(2)}) collective-permute-start(bf16[48,1664]{1,0:T(8,128)(2,1)} %get-tuple-element.309), channel_id=1, source_target_pairs={{0,12},{4,0},{8,4},{12,8},{1,13},{5,1},{9,5},{13,9},{2,14},{6,2},{... | collective-permute-start | bytes 479240 | tf_op jit(solution)/shard_map/ppermute | solution.py:939
  286.7 3.1 fusion
  289.9 3.1 maximum_bitcast_fusion
  303.9 10.4 %collective-permute-done.53 = f32[11,768]{1,0:T(8,128)S(1)} collective-permute-done((f32[11,768]{1,0:T(8,128)S(1)}, f32[11,768]{1,0:T(8,128)S(1)}, u32[]{:S(2)}, u32[]{:S(2)}) %collective-permute-start.53) | collective-permute-done | bytes 33824 | tf_op jit(solution)/shard_map/ppermute | solution.py:952
  317.9 2.5 collective-permute-start.56
  320.5 4.9 %shard_map.211 = (f32[192,3072]{1,0:T(8,128)}, f32[768,768]{1,0:T(8,128)}, f32[192,768]{1,0:T(8,128)}) custom-call(s32[4]{0:T(128)} %pad_add_fusion.idx, bf16[8,432,384]{2,1,0:T(8,128)(2,1)} %bitcast.109), custom_call_target="tpu_custom_call" | custom-call | bytes 7962624 | tf_op jit(solution)/shard_map/pallas_call | solution.py:48
  326.1 3.7 %shard_map.212 = (f32[192,2304]{1,0:T(8,128)}, f32[192,1024]{1,0:T(8,128)}) custom-call(s32[4]{0:T(128)} %pad_add_fusion.idx, bf16[48,1664]{1,0:T(8,128)(2,1)} %copy-done.11, bf16[48,1664]{1,0:T(8,128)(2,1)} %copy-done.30, bf16[48,1664]{1,0:T(8,128)(2,1)} %copy-done.31, bf16[48,1664]{1,0:T(8,128)(2,1)} %copy-done.32, bf16[48,1664]{1,0:T(8,128)(2,1)} %copy-done.33, ...), custom_call_target="tpu_custom_call" | custom-call | bytes 3833856 | tf_op jit(solution)/shard_map/pallas_call | solution.py:48
  (285 shorter events, 96.4 us)
Async XLA Ops:
  7.2 58.0 %all-gather.5.cloned.1.call-start = ((), (), s32[]{:S(2)}) async-start(), calls=%async_computation.2 | async-start | bytes 1658880 | tf_op jit(solution)/shard_map/all_gather | solution.py:884
  16.1 15.4 %collective-permute-start.2 = (bf16[48,1792]{1,0:T(8,128)(2,1)S(1)}, bf16[48,1792]{1,0:T(8,128)(2,1)S(1)}, u32[]{:S(2)}, u32[]{:S(2)}) collective-permute-start(bf16[48,1792]{1,0:T(8,128)(2,1)S(1)} %pad_maximum_fusion.9), channel_id=1, source_target_pairs={{0,8},{4,12},{8,0},{12,4},{1,9},{5,13},{9,1},{13,5},{2,10},{6,14},... | collective-permute-start | bytes 516104 | tf_op jit(solution)/shard_map/ppermute | solution.py:798
  31.5 235.7 %reduce-scatter.2.cloned.1.call-start = ((), (), s32[]{:S(2)}) async-start(), calls=%async_computation.1 | async-start | bytes 1658880 | tf_op jit(solution)/shard_map/reduce_scatter | solution.py:863
  44.5 17.0 %collective-permute-start.10 = (bf16[144,1152]{1,0:T(8,128)(2,1)S(1)}, bf16[144,1152]{1,0:T(8,128)(2,1)S(1)}, u32[]{:S(2)}, u32[]{:S(2)}) collective-permute-start(bf16[144,1152]{1,0:T(8,128)(2,1)S(1)} %slice.88.refs_0_), channel_id=1, source_target_pairs={{0,2},{1,3},{2,0},{3,1},{4,6},{5,7},{6,4},{7,5},{8,10},{9,11},{10,... | collective-permute-start | bytes 995336 | tf_op jit(solution)/shard_map/ppermute | solution.py:802
  46.1 15.4 %collective-permute-start.11 = (bf16[144,1152]{1,0:T(8,128)(2,1)S(1)}, bf16[144,1152]{1,0:T(8,128)(2,1)S(1)}, u32[]{:S(2)}, u32[]{:S(2)}) collective-permute-start(bf16[144,1152]{1,0:T(8,128)(2,1)S(1)} %slice.88.refs_0_), channel_id=1, source_target_pairs={{0,3},{1,2},{2,1},{3,0},{4,7},{5,6},{6,5},{7,4},{8,11},{9,10},{10,... | collective-permute-start | bytes 995336 | tf_op jit(solution)/shard_map/ppermute | solution.py:802
  46.8 15.9 %collective-permute-start.9 = (bf16[144,1152]{1,0:T(8,128)(2,1)S(1)}, bf16[144,1152]{1,0:T(8,128)(2,1)S(1)}, u32[]{:S(2)}, u32[]{:S(2)}) collective-permute-start(bf16[144,1152]{1,0:T(8,128)(2,1)S(1)} %slice.88.refs_0_), channel_id=1, source_target_pairs={{0,1},{1,0},{2,3},{3,2},{4,5},{5,4},{6,7},{7,6},{8,9},{9,8},{10,11... | collective-permute-start | bytes 995336 | tf_op jit(solution)/shard_map/ppermute | solution.py:802
  66.4 28.4 %collective-permute-start.6 = (bf16[720,384]{1,0:T(8,128)(2,1)S(1)}, bf16[720,384]{1,0:T(8,128)(2,1)S(1)}, u32[]{:S(2)}, u32[]{:S(2)}) collective-permute-start(bf16[720,384]{1,0:T(8,128)(2,1)S(1)} %pad_maximum_fusion.6.refs_0_), channel_id=1, source_target_pairs={{0,1},{1,0},{2,3},{3,2},{4,5},{5,4},{6,7},{7,6},{8,9},{9,8},{10,11... | collective-permute-start | bytes 1658888 | tf_op jit(solution)/shard_map/ppermute | solution.py:802
  69.5 26.1 %collective-permute-start.7 = (bf16[720,384]{1,0:T(8,128)(2,1)S(1)}, bf16[720,384]{1,0:T(8,128)(2,1)S(1)}, u32[]{:S(2)}, u32[]{:S(2)}) collective-permute-start(bf16[720,384]{1,0:T(8,128)(2,1)S(1)} %pad_maximum_fusion.6.refs_0_), channel_id=1, source_target_pairs={{0,2},{1,3},{2,0},{3,1},{4,6},{5,7},{6,4},{7,5},{8,10},{9,11},{10,... | collective-permute-start | bytes 1658888 | tf_op jit(solution)/shard_map/ppermute | solution.py:802
  70.4 25.2 %collective-permute-start.8 = (bf16[720,384]{1,0:T(8,128)(2,1)S(1)}, bf16[720,384]{1,0:T(8,128)(2,1)S(1)}, u32[]{:S(2)}, u32[]{:S(2)}) collective-permute-start(bf16[720,384]{1,0:T(8,128)(2,1)S(1)} %pad_maximum_fusion.6.refs_0_), channel_id=1, source_target_pairs={{0,3},{1,2},{2,1},{3,0},{4,7},{5,6},{6,5},{7,4},{8,11},{9,10},{10,... | collective-permute-start | bytes 1658888 | tf_op jit(solution)/shard_map/ppermute | solution.py:802
  96.7 31.6 %collective-permute-start.3 = (bf16[576,384]{1,0:T(8,128)(2,1)}, bf16[576,384]{1,0:T(8,128)(2,1)S(1)}, u32[]{:S(2)}, u32[]{:S(2)}) collective-permute-start(bf16[576,384]{1,0:T(8,128)(2,1)} %pad_maximum_fusion.7.refs_8_), channel_id=1, source_target_pairs={{0,1},{1,0},{2,3},{3,2},{4,5},{5,4},{6,7},{7,6},{8,9},{9,8},{10,11... | collective-permute-start | bytes 1327112 | tf_op jit(solution)/shard_map/ppermute | solution.py:802
  97.6 30.7 %collective-permute-start.4 = (bf16[576,384]{1,0:T(8,128)(2,1)}, bf16[576,384]{1,0:T(8,128)(2,1)S(1)}, u32[]{:S(2)}, u32[]{:S(2)}) collective-permute-start(bf16[576,384]{1,0:T(8,128)(2,1)} %pad_maximum_fusion.7.refs_8_), channel_id=1, source_target_pairs={{0,2},{1,3},{2,0},{3,1},{4,6},{5,7},{6,4},{7,5},{8,10},{9,11},{10,... | collective-permute-start | bytes 1327112 | tf_op jit(solution)/shard_map/ppermute | solution.py:802
  99.1 29.2 %collective-permute-start.5 = (bf16[576,384]{1,0:T(8,128)(2,1)}, bf16[576,384]{1,0:T(8,128)(2,1)S(1)}, u32[]{:S(2)}, u32[]{:S(2)}) collective-permute-start(bf16[576,384]{1,0:T(8,128)(2,1)} %pad_maximum_fusion.7.refs_8_), channel_id=1, source_target_pairs={{0,3},{1,2},{2,1},{3,0},{4,7},{5,6},{6,5},{7,4},{8,11},{9,10},{10,... | collective-permute-start | bytes 1327112 | tf_op jit(solution)/shard_map/ppermute | solution.py:802
  138.6 41.9 %collective-permute-start.28 = (bf16[4,192,384]{2,1,0:T(8,128)(2,1)S(1)}, bf16[4,192,384]{2,1,0:T(8,128)(2,1)S(1)}, u32[]{:S(2)}, u32[]{:S(2)}) collective-permute-start(bf16[4,192,384]{2,1,0:T(8,128)(2,1)S(1)} %get-tuple-element.300), channel_id=1, source_target_pairs={{0,1},{1,0},{2,3},{3,2},{4,5},{5,4},{6,7},{7,6},{8,9},{9,8},{10,11... | collective-permute-start | bytes 1769480 | tf_op jit(solution)/shard_map/ppermute | solution.py:860
  139.6 40.9 %collective-permute-start.29 = (bf16[4,192,384]{2,1,0:T(8,128)(2,1)S(1)}, bf16[4,192,384]{2,1,0:T(8,128)(2,1)S(1)}, u32[]{:S(2)}, u32[]{:S(2)}) collective-permute-start(bf16[4,192,384]{2,1,0:T(8,128)(2,1)S(1)} %get-tuple-element.299), channel_id=1, source_target_pairs={{0,2},{1,3},{2,0},{3,1},{4,6},{5,7},{6,4},{7,5},{8,10},{9,11},{10,... | collective-permute-start | bytes 1769480 | tf_op jit(solution)/shard_map/ppermute | solution.py:860
  141.0 39.5 %collective-permute-start.30 = (bf16[4,192,384]{2,1,0:T(8,128)(2,1)S(1)}, bf16[4,192,384]{2,1,0:T(8,128)(2,1)S(1)}, u32[]{:S(2)}, u32[]{:S(2)}) collective-permute-start(bf16[4,192,384]{2,1,0:T(8,128)(2,1)S(1)} %get-tuple-element.298), channel_id=1, source_target_pairs={{0,3},{1,2},{2,1},{3,0},{4,7},{5,6},{6,5},{7,4},{8,11},{9,10},{10,... | collective-permute-start | bytes 1769480 | tf_op jit(solution)/shard_map/ppermute | solution.py:860
  191.9 42.5 %collective-permute-start.39 = (bf16[4,240,384]{2,1,0:T(8,128)(2,1)}, bf16[4,240,384]{2,1,0:T(8,128)(2,1)}, u32[]{:S(2)}, u32[]{:S(2)}) collective-permute-start(bf16[4,240,384]{2,1,0:T(8,128)(2,1)} %pad_maximum_fusion.5), channel_id=1, source_target_pairs={{0,3},{1,2},{2,1},{3,0},{4,7},{5,6},{6,5},{7,4},{8,11},{9,10},{10,... | collective-permute-start | bytes 2211848 | tf_op jit(solution)/shard_map/ppermute | solution.py:860
  194.6 39.7 %collective-permute-start.38 = (bf16[4,240,384]{2,1,0:T(8,128)(2,1)}, bf16[4,240,384]{2,1,0:T(8,128)(2,1)S(1)}, u32[]{:S(2)}, u32[]{:S(2)}) collective-permute-start(bf16[4,240,384]{2,1,0:T(8,128)(2,1)} %pad_maximum_fusion.4), channel_id=1, source_target_pairs={{0,2},{1,3},{2,0},{3,1},{4,6},{5,7},{6,4},{7,5},{8,10},{9,11},{10,... | collective-permute-start | bytes 2211848 | tf_op jit(solution)/shard_map/ppermute | solution.py:860
  196.1 38.2 %collective-permute-start.37 = (bf16[4,240,384]{2,1,0:T(8,128)(2,1)}, bf16[4,240,384]{2,1,0:T(8,128)(2,1)}, u32[]{:S(2)}, u32[]{:S(2)}) collective-permute-start(bf16[4,240,384]{2,1,0:T(8,128)(2,1)} %pad_maximum_fusion.3), channel_id=1, source_target_pairs={{0,1},{1,0},{2,3},{3,2},{4,5},{5,4},{6,7},{7,6},{8,9},{9,8},{10,11... | collective-permute-start | bytes 2211848 | tf_op jit(solution)/shard_map/ppermute | solution.py:860
  237.7 82.7 %all-gather.7.cloned.1.call-start = ((), (), s32[]{:S(2)}) async-start(), calls=%async_computation.3 | async-start | bytes 2985984 | tf_op jit(solution)/shard_map/all_gather | solution.py:936
  243.5 23.7 %collective-permute-start.41 = (bf16[4,48,1664]{2,1,0:T(8,128)(2,1)}, bf16[4,48,1664]{2,1,0:T(8,128)(2,1)}, u32[]{:S(2)}, u32[]{:S(2)}) collective-permute-start(bf16[4,48,1664]{2,1,0:T(8,128)(2,1)} %get-tuple-element.292), channel_id=1, source_target_pairs={{0,1},{1,0},{2,3},{3,2},{4,5},{5,4},{6,7},{7,6},{8,9},{9,8},{10,11... | collective-permute-start | bytes 1916936 | tf_op jit(solution)/shard_map/ppermute | solution.py:860
  244.4 29.2 %collective-permute-start.42 = (bf16[4,48,1664]{2,1,0:T(8,128)(2,1)}, bf16[4,48,1664]{2,1,0:T(8,128)(2,1)}, u32[]{:S(2)}, u32[]{:S(2)}) collective-permute-start(bf16[4,48,1664]{2,1,0:T(8,128)(2,1)} %get-tuple-element.291), channel_id=1, source_target_pairs={{0,2},{1,3},{2,0},{3,1},{4,6},{5,7},{6,4},{7,5},{8,10},{9,11},{10,... | collective-permute-start | bytes 1916936 | tf_op jit(solution)/shard_map/ppermute | solution.py:860
  245.9 28.7 %collective-permute-start.43 = (bf16[4,48,1664]{2,1,0:T(8,128)(2,1)}, bf16[4,48,1664]{2,1,0:T(8,128)(2,1)}, u32[]{:S(2)}, u32[]{:S(2)}) collective-permute-start(bf16[4,48,1664]{2,1,0:T(8,128)(2,1)} %get-tuple-element.290), channel_id=1, source_target_pairs={{0,3},{1,2},{2,1},{3,0},{4,7},{5,6},{6,5},{7,4},{8,11},{9,10},{10,... | collective-permute-start | bytes 1916936 | tf_op jit(solution)/shard_map/ppermute | solution.py:860
  282.3 14.3 %collective-permute-start.45 = (bf16[48,1664]{1,0:T(8,128)(2,1)}, bf16[48,1664]{1,0:T(8,128)(2,1)S(1)}, u32[]{:S(2)}, u32[]{:S(2)}) collective-permute-start(bf16[48,1664]{1,0:T(8,128)(2,1)} %get-tuple-element.310), channel_id=1, source_target_pairs={{0,4},{4,8},{8,12},{12,0},{1,5},{5,9},{9,13},{13,1},{2,6},{6,10},{... | collective-permute-start | bytes 479240 | tf_op jit(solution)/shard_map/ppermute | solution.py:939
  298.9 15.4 %collective-permute-start.50 = (bf16[48,1664]{1,0:T(8,128)(2,1)S(1)}, bf16[48,1664]{1,0:T(8,128)(2,1)S(1)}, u32[]{:S(2)}, u32[]{:S(2)}) collective-permute-start(bf16[48,1664]{1,0:T(8,128)(2,1)S(1)} %add_convert_fusion.7.refs_0_), channel_id=1, source_target_pairs={{0,1},{1,0},{2,3},{3,2},{4,5},{5,4},{6,7},{7,6},{8,9},{9,8},{10,11... | collective-permute-start | bytes 479240 | tf_op jit(solution)/shard_map/ppermute | solution.py:802
  (95 other events, 895.9 us)
Sparse Core Ops, SparseCore 0:
  31.6 32.2 all-gather.4
  237.9 29.3 reduce-scatter.1
  281.3 35.5 all-gather.6
where the time goes:
time: 342 us; the launch traced here: 338 us
  Pallas kernels  157 us (46%)
  waiting for transfers between devices  61.7 us (18%)
  starting transfers between devices  50.5 us (15%)
  other arithmetic  34.5 us (10%)
  local copies, waits for them, and re-layouts  19.7 us (6%)
  between operations  15 us (4%)
    pallas_call x9, Pallas kernels, call(): pl.pallas_call(kernel, grid_spec=spec, out_shape=out_shape, compiler_para...  157 us
    ppermute x15, starting transfers between devices, over_plane(): return [near] + [lax.ppermute(near, 'dp', flip(e)) for e in (1, 2, 3)]  17.7 us
    convert_element_type x8, other arithmetic, total(): return out.astype(bf16)  12.5 us
    ppermute x4, waiting for transfers between devices, both_cores(): return total([near, lax.ppermute(away, 'section', SWAP)])  12.5 us
    ppermute x3, waiting for transfers between devices, over_line(): lax.ppermute(piece, 'chan', shift(k))  11.6 us
    ppermute x15, waiting for transfers between devices, over_plane(): return [near] + [lax.ppermute(near, 'dp', flip(e)) for e in (1, 2, 3)]  11.1 us
    ppermute x9, starting transfers between devices, to_plane(): lax.ppermute(parts[e], 'dp', flip(e))  10.5 us
    ppermute x1, waiting for transfers between devices, fast_body(): tiny += lax.ppermute(tiny, 'dp', flip(2))  10.4 us
  transfers between devices with their start and end apart: 64, of which 19 were waited for; matrix products, arithmetic and copies ran while one was open for 10% of the time, Pallas kernels for 46%

commit v1 on v0

--- a/solution.py
+++ b/solution.py
@@ -154,7 +154,7 @@
 
 
 def spectra_kernel(idx, *refs):
-    held, (own_taps, own_small, basis_ref, out_ref, small_ref, taps_ref, taps, small, tall, sig, sems, sems2) = refs[:8], refs[8:]
+    held, (own_taps, own_small, basis_in, out_ref, small_ref, taps_ref, taps, small, tall, sig, basis_ref, sems, sems2, sem_b) = refs[:8], refs[8:]
     mine, other = held[:4], held[4:]
     length = taps.shape[1]
 
@@ -169,16 +169,18 @@
                 z = lax.rem(idx[0] + 4 - k, 4)
                 copies2.append((mine[e].at[pl.ds(j * r, r), pl.ds(REST_SMALL, 128)],
                                 small.at[pl.ds(pl.multiple_of(z * part + (idx[1] ^ e) * r, 16), r), :]))
+        start_all(copies2, sems2)
         start_all(copies, sems)
-        start_all(copies2, sems2)
+        start_all([(basis_in, basis_ref)], sem_b)
         wait_all(copies2, sems2)
-        wait_all(copies, sems)
         wide = small[...].astype(f32)
         small_ref[...] = wide.T[0:8]
         for z in range(4):
             for q in range(3):
                 tall[(3 * z + q) * part : (3 * z + q + 1) * part] = pltpu.roll(wide[z * part : (z + 1) * part], 126 - q, 1)
         taps_ref[...] = tall[...].T[0:8]
+        wait_all(copies, sems)
+        wait_all([(basis_in, basis_ref)], sem_b)
 
     position = lax.broadcasted_iota(jnp.int32, (1, length), 1).astype(f32)
     rows = pl.ds(pl.multiple_of(pl.program_id(0) * CH, CH), CH)
@@ -195,10 +197,11 @@
     return call(
         spectra_kernel,
         (width // CH,),
-        [ANY] * 10 + [whole(basis.shape)],
+        [ANY] * 11,
         [cols_of(2 * length, CH), whole((8, width)), whole((8, 3 * width))],
         [sds((2 * length, width), bf16), sds((8, width), f32), sds((8, 3 * width), f32)],
-        [pltpu.VMEM((width, length), bf16), pltpu.VMEM((width, 128), bf16), pltpu.VMEM((3 * width, 128), f32), pltpu.VMEM((CH, length), bf16), SEMS, SEMS],
+        [pltpu.VMEM((width, length), bf16), pltpu.VMEM((width, 128), bf16), pltpu.VMEM((3 * width, 128), f32), pltpu.VMEM((CH, length), bf16),
+         pltpu.VMEM(basis.shape, bf16), SEMS, SEMS, pltpu.SemaphoreType.DMA((1,))],
         (idx, *rest, own_taps, own_small, basis),
         4 * length * length * width,
         basis.size * 2 + 6 * length * width,
@@ -450,31 +453,37 @@
 
 
 def down_kernel(idx, *refs):
-    held, (own_up, own_down, og_ref, act0_ref, normed_ref, hidden_ref, slope_ref, gated_ref, gain_ref,
-           act1_ref, ag_ref, branch_ref, gg_ref, near_ref, away_ref, near_out, away_out,
-           wu_ref, wd_ref, acc, gn, branch, turned, sem_u, sem_d) = refs[:16], refs[16:]
+    held, (own_up, own_down, act0_in, normed_in, gated_in, og_ref, slope_ref, gain_ref,
+           ag_ref, branch_ref, gg_ref, near_ref, away_ref, near_out, away_out,
+           wu_ref, wd_ref, gn, branch, turned, act0_ref, normed_ref, gated_ref, sem_u, sem_d, sem_l, sem_m) = refs[:16], refs[16:]
     length, width = og_ref.shape
     half = width // 2
     c = pl.program_id(0)
     live = live_rows(idx, length)
+    ups = up_copies(idx, own_up, held[:4], held[4:8], wu_ref)
+    late = [(normed_in, normed_ref), (act0_in, act0_ref), (gated_in, gated_ref)]
 
     @pl.when(c == 0)
     def _():
-        ups = up_copies(idx, own_up, held[:4], held[4:8], wu_ref)
         downs = down_copies(idx, own_down, held[8:12], held[12:], wd_ref)
         start_all(downs, sem_d)
-        start_all(ups, sem_u)
         branch[...] = (live * og_ref[...].astype(f32)).astype(bf16)
-        acc[...] = act0_ref[...].astype(f32)
         gn[...] = jnp.zeros((length, width), f32)
         wait_all(downs, sem_d)
-        wait_all(ups, sem_u)
+        start_all(ups, sem_u)
+        start_all(late[:1], sem_l)
 
     at = pl.ds(pl.multiple_of(c * width, width), width)
     pre = (slope_ref[...].astype(f32) * dot(branch[...], wd_ref[at, :], 1, 1)).astype(bf16)
     for n, cols in enumerate(near_first(idx, turned, half)):
         turned[:, cols] = pre[:, n * half : (n + 1) * half]
-    acc[...] += dot(hidden_ref[...], wd_ref[at, :])
+
+    @pl.when(c == 0)
+    def _():
+        wait_all(ups, sem_u)
+        wait_all(late[:1], sem_l)
+        start_all(late[1:], sem_m)
+
     gn[...] += dot(pre, wu_ref[:, at], 1, 1)
     grad = dot(normed_ref[...], turned[...], 0, 0).astype(bf16)
     near_ref[...] = grad[:, :half]
@@ -482,7 +491,7 @@
 
     @pl.when(c == pl.num_programs(0) - 1)
     def _():
-        act1_ref[...] = (live * acc[...]).astype(bf16)
+        wait_all(late[1:], sem_m)
         hat, inv = norm_parts(act0_ref[...].astype(f32))
         gg_ref[...] = jnp.sum(gn[...] * hat, axis=0, keepdims=True)
         ag = live * og_ref[...].astype(f32) + norm_back(gn[...], hat, inv, gain_ref[...])
@@ -495,7 +504,7 @@
         away_out[...] = g_out[:, half:]
 
 
-def mlp_down(idx, held_up, held_down, own_up, own_down, og, act0, normed, hidden, slope, gated, gain):
+def mlp_down(idx, held_up, held_down, own_up, own_down, og, act0, normed, slope, gated, gain):
     length, width = act0.shape
     ff = own_up.shape[1]
     half = width // 2
@@ -508,14 +517,52 @@
     return call(
         down_kernel,
         (ff // width,),
-        [ANY] * 18 + [picked, one, one, wide, wide, one, whole(gain.shape)],
-        [one, one, one, whole((1, width)), cols_of(width, half), cols_of(width, half), whole((width, half)), whole((width, half))],
-        [full, sds((length, width), f32), full, sds((1, width), f32), sds((width, ff // 2), bf16), sds((width, ff // 2), bf16),
+        [ANY] * 21 + [picked, wide, whole(gain.shape)],
+        [one, one, whole((1, width)), cols_of(width, half), cols_of(width, half), whole((width, half)), whole((width, half))],
+        [sds((length, width), f32), full, sds((1, width), f32), sds((width, ff // 2), bf16), sds((width, ff // 2), bf16),
          sds((width, half), bf16), sds((width, half), bf16)],
-        [pltpu.VMEM((width, ff), bf16), pltpu.VMEM((ff, width), bf16), col, col, low, low, SEMS, SEMS],
-        (idx, *held_up, *held_down, own_up, own_down, og, act0, normed, hidden, slope, gated, gain),
-        8 * length * width * ff,
-        2 * (8 * length * width + 3 * width * ff + 2 * length * ff),
+        [pltpu.VMEM((width, ff), bf16), pltpu.VMEM((ff, width), bf16), col, low, low, low, low, low, SEMS, SEMS,
+         pltpu.SemaphoreType.DMA((1,)), pltpu.SemaphoreType.DMA((2,))],
+        (idx, *held_up, *held_down, own_up, own_down, act0, normed, gated, og, slope, gain),
+        6 * length * width * ff,
+        2 * (7 * length * width + 3 * width * ff + length * ff),
+        prefetch=1,
+    )
+
+
+def last_kernel(idx, *refs):
+    held, (own_down, hidden_ref, act0_ref, act1_ref, wd_ref, acc, sem_d) = refs[:8], refs[8:]
+    length, width = act0_ref.shape
+    c = pl.program_id(0)
+
+    @pl.when(c == 0)
+    def _():
+        downs = down_copies(idx, own_down, held[:4], held[4:], wd_ref)
+        start_all(downs, sem_d)
+        acc[...] = act0_ref[...].astype(f32)
+        wait_all(downs, sem_d)
+
+    acc[...] += dot(hidden_ref[...], wd_ref[pl.ds(pl.multiple_of(c * width, width), width), :])
+
+    @pl.when(c == pl.num_programs(0) - 1)
+    def _():
+        act1_ref[...] = (live_rows(idx, length) * acc[...]).astype(bf16)
+
+
+def mlp_last(idx, held, own_down, hidden, act0):
+    length, width = act0.shape
+    ff = own_down.shape[0] * 4
+    one = whole((length, width))
+    return call(
+        last_kernel,
+        (ff // width,),
+        [ANY] * 9 + [cols_of(length, width), one],
+        one,
+        sds((length, width), bf16),
+        [pltpu.VMEM((ff, width), bf16), pltpu.VMEM((length, width), f32), SEMS],
+        (idx, *held, own_down, hidden, act0),
+        2 * length * width * ff,
+        2 * (2 * length * width + width * ff + length * ff),
         prefetch=1,
     )
 
@@ -905,10 +952,10 @@
     h_down = both_cores(near, away).reshape(4, 4, part, half)
     sent_down = [lax.dynamic_index_in_dim(h_down, d ^ e, 1, keepdims=False) for e in range(4)]
     got_down = to_plane(sent_down)
-    got_down, (act1, ag1, branch0, g_gain_mlp, near, away, near_out, away_out) = after(
+    got_down, (ag1, branch0, g_gain_mlp, near, away, near_out, away_out) = after(
         got_down,
         mlp_down(
-            idx, held_up, held_down, own_up, own_down, og, act0, normed1, hidden, tie(slope, *sent_down), gated, gain_mlp
+            idx, held_up, held_down, own_up, own_down, og, act0, normed1, tie(slope, *sent_down), gated, gain_mlp
         ),
     )
     h_up = both_cores(near, away).reshape(4, part, ff // 2)
@@ -930,17 +977,19 @@
     sent_mix = [lax.dynamic_index_in_dim(h_mix, d ^ e, 1, keepdims=False) for e in range(4)]
     got_mix = to_plane(sent_mix)
     ag0, g_gain_mix = input_backward(idx, held_in, own_in, tie(g_mixed, u_mlp, *sent_mix), x, branch0, gain_mix)
+    act1 = mlp_last(idx, held_down, own_down, hidden, tie(act0, ag0))
     tiny = jnp.concatenate([g_gain_mix, g_gain_mlp, g_taps], 0)
     tiny += lax.ppermute(tiny, "section", SWAP)
-    (*got_mix, p_mlp), (ag0, tiny) = after([*got_mix, p_mlp], [ag0, tiny])
+    swapped = jnp.concatenate([jnp.where(first, act1, act0), jnp.where(first, ag1, ag0).astype(bf16)], 0)
+    (*got_mix, p_mlp), (ag0, tiny, swapped) = after([*got_mix, p_mlp], [ag0, tiny, swapped])
     all_mlp = lax.all_gather(p_mlp, ("dp", "section"), axis=0)
     u_mix = total(got_mix)
     sent_line = [lax.dynamic_index_in_dim(u_mix, (z + k) % 4, 0, keepdims=False) for k in (0, *SHIFTS)]
     got_line = [sent_line[0]] + [lax.ppermute(v, "chan", shift(k)) for k, v in zip(SHIFTS, sent_line[1:])]
     tiny = tie(tiny, *sent_line)
     tiny += lax.ppermute(tiny, "dp", flip(1))
+    tiny += lax.ppermute(tiny, "dp", flip(2))
     ag0_late = tie(ag0, *sent_line)
-    swapped = jnp.concatenate([jnp.where(first, act1, act0), jnp.where(first, ag1, ag0_late).astype(bf16)], 0)
     swapped = lax.ppermute(swapped, "section", SWAP)
     out_act = stacked(act0, act1, swapped[:length], bf16)
     out_ag = stacked(ag0_late, ag1, swapped[length:], f32)
@@ -949,13 +998,13 @@
     p_mix = total(got_line)
     plane_mix = over_plane(p_mix)
     tiny = tie(tiny, p_mix)
-    tiny += lax.ppermute(tiny, "dp", flip(2))
+    tiny += lax.ppermute(tiny, "chan", flip(1))
     plane_mix, (tiny,) = after(plane_mix, [tiny])
-    got_tiny = [lax.ppermute(tiny, "chan", flip(e)) for e in (1, 2, 3)]
+    got_tiny = [lax.ppermute(tiny, "chan", flip(2))]
     held_mix, (g_up, g_down, g_out) = after(over_chip(plane_mix), [g_up, g_down, g_out])
     g_in, g_kern = unpack(unpack_mix_kernel, idx, held_mix, [(part, 3 * width), (part, length)])
     got_tiny, (g_in, g_kern) = after(got_tiny, [g_in, g_kern])
-    tiny = (tiny + got_tiny[0]) + (got_tiny[1] + got_tiny[2])
+    tiny += got_tiny[0]
 
     mine = cut(tiny[0:2], z * part, part, 1)
     g_taps = tiny[2:11].reshape(3, 3, width).transpose(1, 0, 2).reshape(3, 3 * width)

time: 342 us -> 331 us (0.968)
  waiting for transfers between devices: 61.7 us -> 47.4 us
  Pallas kernels: 157 us -> 161 us
    ppermute x1, waiting for transfers between devices: 10.4 us -> 0.01 us  [fast_body(): tiny += lax.ppermute(tiny, 'dp', flip(2))]
    ppermute x9, waiting for transfers between devices: 7.44 us -> 0.02 us  [to_plane(): lax.ppermute(parts[e], 'dp', flip(e))]
    reduce_scatter x1, waiting for transfers between devices: 5.56 us -> 0.02 us  [line_sum(): return lax.psum_scatter(held, 'chan', scatter_dimension=0, tiled=False)]
    pallas_call x9 -> x10, Pallas kernels: 157 us -> 161 us  [call(): pl.pallas_call(kernel, grid_spec=spec, out_shape=out_shape, compiler_para...]
    ppermute x3 -> x2, waiting for transfers between devices: 0.01 us -> 4.09 us  [the longest x1 4.09 us: fast_body(): tiny += lax.ppermute(tiny, 'chan', flip(1))]
    ppermute x15, waiting for transfers between devices: 11.1 us -> 15.1 us  [over_plane(): return [near] + [lax.ppermute(near, 'dp', flip(e)) for e in (1, 2, 3)]]
  transfers between devices with their start and end apart: 64 -> 63, of which waited for: 19 -> 15; matrix products, arithmetic and copies ran while one was open for 10% -> 12% of each run, Pallas kernels for 46% -> 49%
where the time goes in v1:
time: 331 us; the launch traced here: 326 us
  Pallas kernels  161 us (49%)
  starting transfers between devices  48.7 us (15%)
  waiting for transfers between devices  47.4 us (14%)
  other arithmetic  35 us (11%)
  local copies, waits for them, and re-layouts  19.2 us (6%)
  between operations  15 us (5%)
    pallas_call x10, Pallas kernels, call(): pl.pallas_call(kernel, grid_spec=spec, out_shape=out_shape, compiler_para...  161 us
    ppermute x15, starting transfers between devices, over_plane(): return [near] + [lax.ppermute(near, 'dp', flip(e)) for e in (1, 2, 3)]  17.7 us
    ppermute x15, waiting for transfers between devices, over_plane(): return [near] + [lax.ppermute(near, 'dp', flip(e)) for e in (1, 2, 3)]  15.1 us
    convert_element_type x8, other arithmetic, total(): return out.astype(bf16)  13.8 us
    ppermute x3, waiting for transfers between devices, over_line(): lax.ppermute(piece, 'chan', shift(k))  11.6 us
    ppermute x4, waiting for transfers between devices, both_cores(): return total([near, lax.ppermute(away, 'section', SWAP)])  11.4 us
    ppermute x9, starting transfers between devices, to_plane(): lax.ppermute(parts[e], 'dp', flip(e))  10.5 us
  transfers between devices with their start and end apart: 63, of which 15 were waited for; matrix products, arithmetic and copies ran while one was open for 12% of the time, Pallas kernels for 49%

profile of v1, /device:TPU:0, one launch (start us, length us, event | category | flops | bytes accessed | tf_op | source)
XLA Modules:
  0.0 326.4 jit_solution(7706019236623901430)
XLA Ops:
  10.9 3.1 collective-permute-start
  23.5 7.9 %collective-permute-done.2 = bf16[48,1792]{1,0:T(8,128)(2,1)S(1)} collective-permute-done((bf16[48,1792]{1,0:T(8,128)(2,1)S(1)}, bf16[48,1792]{1,0:T(8,128)(2,1)S(1)}, u32[]{:S(2)}, u32[]{:S(2)}) %collective-permute-start.2) | collective-permute-done | bytes 172064 | tf_op jit(solution)/shard_map/ppermute | solution.py:845
  35.1 4.0 %collective-permute-done.12.refs_1_ = bf16[144,640]{1,0:T(8,128)(2,1)S(1)} collective-permute-done((bf16[144,640]{1,0:T(8,128)(2,1)S(1)}, bf16[144,640]{1,0:T(8,128)(2,1)S(1)}, u32[]{:S(2)}, u32[]{:S(2)}) %collective-permute-start.12) | collective-permute-done | bytes 184352 | tf_op jit(solution)/shard_map/ppermute | solution.py:849
  39.2 4.2 %collective-permute-done.13.refs_2_ = bf16[144,640]{1,0:T(8,128)(2,1)S(1)} collective-permute-done((bf16[144,640]{1,0:T(8,128)(2,1)S(1)}, bf16[144,640]{1,0:T(8,128)(2,1)S(1)}, u32[]{:S(2)}, u32[]{:S(2)}) %collective-permute-start.13) | collective-permute-done | bytes 184352 | tf_op jit(solution)/shard_map/ppermute | solution.py:849
  50.7 9.4 %shard_map.204 = (bf16[2048,768]{1,0:T(8,128)(2,1)}, f32[8,768]{1,0:T(8,128)}, f32[8,2304]{1,0:T(8,128)}) custom-call(s32[4]{0:T(128)} %pad_add_fusion.idx, bf16[144,640]{1,0:T(8,128)(2,1)} %copy-done.28, bf16[144,640]{1,0:T(8,128)(2,1)} %copy-done.47, bf16[144,640]{1,0:T(8,128)(2,1)} %copy-done.48, bf16[144,640]{1,0:T(8,128)(2,1)} %copy-done.49, ...), custom_call_target="tpu_custom_call" | custom-call | flops 3221225472 | bytes 8912896 | tf_op jit(solution)/shard_map/pallas_call | solution.py:48
  71.9 22.8 %shard_map.205 = (bf16[1024,768]{1,0:T(8,128)(2,1)}, bf16[3,1024,768]{2,1,0:T(8,128)(2,1)}, bf16[3,1024,768]{2,1,0:T(8,128)(2,1)}, bf16[2048,768]{1,0:T(8,128)(2...) custom-call(s32[4]{0:T(128)} %pad_add_fusion.idx, bf16[144,1152]{1,0:T(8,128)(2,1)} %copy-done.25, ...), custom_call_target="tpu_custom_call" | custom-call | flops 10066329600 | bytes 37093376 | tf_op jit(solution)/shard_map/pallas_call | solution.py:48
  101.3 7.0 %shard_map.206 = (bf16[1024,768]{1,0:T(8,128)(2,1)}, bf16[1024,768]{1,0:T(8,128)(2,1)}) custom-call(s32[4]{0:T(128)} %pad_add_fusion.idx, bf16[720,384]{1,0:T(8,128)(2,1)} %copy-done.10, bf16[720,384]{1,0:T(8,128)(2,1)} %copy-done.17, bf16[720,384]{1,0:T(8,128)(2,1)} %copy-done.18, bf16[720,384]{1,0:T(8,128)(2,1)} %copy-done.19, ...), custom_call_target="tpu_custom_call" | custom-call | flops 1207959552 | bytes 7471104 | tf_op jit(solution)/shard_map/pallas_call | solution.py:48
  108.3 19.9 %shard_map.207 = (bf16[1024,3072]{1,0:T(8,128)(2,1)}, bf16[1024,3072]{1,0:T(8,128)(2,1)}, bf16[3072,384]{1,0:T(8,128)(2,1)}, bf16[3072,384]{1,0:T(8,128)(2,1)}) custom-call(s32[4]{0:T(128)} %pad_add_fusion.idx, bf16[720,384]{1,0:T(8,128)(2,1)} %copy-done.10, bf16[720,384]{1,0:T(8,128)(2,1)} %copy-done.17, bf16[720,384]{1,0:T(8,128)(2,1)} %copy-done.18, ...), custom_call_target="tpu_custom_call" | custom-call | flops 9663676416 | bytes 25165824 | tf_op jit(solution)/shard_map/pallas_call | solution.py:48
  130.4 5.6 %collective-permute-done.27 = bf16[3072,384]{1,0:T(8,128)(2,1)S(1)} collective-permute-done((bf16[3072,384]{1,0:T(8,128)(2,1)}, bf16[3072,384]{1,0:T(8,128)(2,1)S(1)}, u32[]{:S(2)}, u32[]{:S(2)}) %collective-permute-start.27) | collective-permute-done | bytes 2359328 | tf_op jit(solution)/shard_map/ppermute | solution.py:898
  142.2 31.4 %shard_map.208 = (f32[1024,768]{1,0:T(8,128)}, bf16[1024,768]{1,0:T(8,128)(2,1)}, f32[1,768]{1,0:T(1,128)}, bf16[768,1536]{1,0:T(8,128)(2,1)}, bf16[768,1536]{1,...) custom-call(s32[4]{0:T(128)} %pad_add_fusion.idx, bf16[720,384]{1,0:T(8,128)(2,1)} %copy-done.10, ...), custom_call_target="tpu_custom_call" | custom-call | flops 14495514624 | bytes 31457280 | tf_op jit(solution)/shard_map/pallas_call | solution.py:48
  174.9 5.1 %collective-permute-done.36 = bf16[768,384]{1,0:T(8,128)(2,1)S(1)} collective-permute-done((bf16[768,384]{1,0:T(8,128)(2,1)}, bf16[768,384]{1,0:T(8,128)(2,1)S(1)}, u32[]{:S(2)}, u32[]{:S(2)}) %collective-permute-start.36) | collective-permute-done | bytes 589856 | tf_op jit(solution)/shard_map/ppermute | solution.py:898
  181.4 2.4 add_convert_fusion.1
  190.4 37.0 %shard_map.209 = (bf16[3,1024,768]{2,1,0:T(8,128)(2,1)}, bf16[768,1664]{1,0:T(8,128)(2,1)}, bf16[768,1664]{1,0:T(8,128)(2,1)}, f32[9,768]{1,0:T(8,128)}) custom-call(s32[4]{0:T(128)} %pad_add_fusion.idx, bf16[720,384]{1,0:T(8,128)(2,1)} %copy-done.10, bf16[720,384]{1,0:T(8,128)(2,1)} %copy-done.17, bf16[720,384]{1,0:T(8,128)(2,1)} %copy-done.18, ...), custom_call_target="tpu_custom_call" | custom-call | flops 14495514624 | bytes 48103424 | tf_op jit(solution)/shard_map/pallas_call | solution.py:48
  232.9 2.4 add_convert_fusion
  240.4 12.1 %shard_map.210 = (f32[1024,768]{1,0:T(8,128)}, f32[1,768]{1,0:T(1,128)}) custom-call(s32[4]{0:T(128)} %pad_add_fusion.idx, bf16[144,1152]{1,0:T(8,128)(2,1)} %copy-done.25, bf16[144,1152]{1,0:T(8,128)(2,1)} %copy-done.45, bf16[144,1152]{1,0:T(8,128)(2,1)} %copy-done.43, bf16[144,1152]{1,0:T(8,128)(2,1)} %copy-done.44, bf16[144,1152]{1,0:T(8,128)(2,1)} %copy-done.46, ...), custom_call_target="tpu_custom_call" | custom-call | flops 3623878656 | bytes 14548992 | tf_op jit(solution)/shard_map/pallas_call | solution.py:48
  252.5 12.8 %shard_map.211 = bf16[1024,768]{1,0:T(8,128)(2,1)} custom-call(s32[4]{0:T(128)} %pad_add_fusion.idx, bf16[576,384]{1,0:T(8,128)(2,1)} %pad_maximum_fusion.7.refs_8_.refs_0_, bf16[576,384]{1,0:T(8,128)(2,1)} %copy-done.38, bf16[576,384]{1,0:T(8,128)(2,1)} %copy-done.39, bf16[576,384]{1,0:T(8,128)(2,1)} %copy-done.40, bf16[576,384]{1,0:T(8,128)(2,1)} %copy-done.41, ...), custom_call_target="tpu_custom_call" | custom-call | flops 4831838208 | bytes 14155776 | tf_op jit(solution)/shard_map/pallas_call | solution.py:48
  274.3 3.2 collective-permute-done.48
  278.9 4.1 %collective-permute-start.46 = (bf16[48,1664]{1,0:T(8,128)(2,1)S(1)}, bf16[48,1664]{1,0:T(8,128)(2,1)S(1)}, u32[]{:S(2)}, u32[]{:S(2)}) collective-permute-start(bf16[48,1664]{1,0:T(8,128)(2,1)S(1)} %get-tuple-element.305), channel_id=1, source_target_pairs={{0,12},{4,0},{8,4},{12,8},{1,13},{5,1},{9,5},{13,9},{2,14},{6,2},{... | collective-permute-start | bytes 479240 | tf_op jit(solution)/shard_map/ppermute | solution.py:988
  285.0 3.5 %maximum_bitcast_fusion = f32[1,2,1,1024,768]{4,3,1,2,0:T(8,128)} fusion(f32[1,1024,768]{2,1,0:T(8,128)S(1)} %get-tuple-element.283, f32[1,1024,768]{2,1,0:T(8,128)S(1)} %get-tuple-element.282), kind=kLoop, calls=%fused_computation | loop fusion | flops 1572864 | bytes 12582912 | tf_op jit(solution)/shard_map/broadcast_in_dim | solution.py:904
  297.8 4.1 %collective-permute-done.54 = f32[11,768]{1,0:T(8,128)S(1)} collective-permute-done((f32[11,768]{1,0:T(8,128)S(1)}, f32[11,768]{1,0:T(8,128)S(1)}, u32[]{:S(2)}, u32[]{:S(2)}) %collective-permute-start.54) | collective-permute-done | bytes 33824 | tf_op jit(solution)/shard_map/ppermute | solution.py:1001
  301.9 3.4 %collective-permute-done.53.refs_3_ = bf16[48,1664]{1,0:T(8,128)(2,1)S(1)} collective-permute-done((bf16[48,1664]{1,0:T(8,128)(2,1)S(1)}, bf16[48,1664]{1,0:T(8,128)(2,1)S(1)}, u32[]{:S(2)}, u32[]{:S(2)}) %collective-permute-start.53) | collective-permute-done | bytes 159776 | tf_op jit(solution)/shard_map/ppermute | solution.py:849
  306.3 2.4 collective-permute-start.55
  308.8 4.9 %shard_map.212 = (f32[192,3072]{1,0:T(8,128)}, f32[768,768]{1,0:T(8,128)}, f32[192,768]{1,0:T(8,128)}) custom-call(s32[4]{0:T(128)} %pad_add_fusion.idx, bf16[8,432,384]{2,1,0:T(8,128)(2,1)} %bitcast.109), custom_call_target="tpu_custom_call" | custom-call | bytes 7962624 | tf_op jit(solution)/shard_map/pallas_call | solution.py:48
  314.5 3.7 %shard_map.213 = (f32[192,2304]{1,0:T(8,128)}, f32[192,1024]{1,0:T(8,128)}) custom-call(s32[4]{0:T(128)} %pad_add_fusion.idx, bf16[48,1664]{1,0:T(8,128)(2,1)} %copy-done.11, bf16[48,1664]{1,0:T(8,128)(2,1)} %copy-done.29, bf16[48,1664]{1,0:T(8,128)(2,1)} %copy-done.30, bf16[48,1664]{1,0:T(8,128)(2,1)} %copy-done.31, bf16[48,1664]{1,0:T(8,128)(2,1)} %copy-done.32, ...), custom_call_target="tpu_custom_call" | custom-call | bytes 3833856 | tf_op jit(solution)/shard_map/pallas_call | solution.py:48
  (283 shorter events, 94.9 us)
Async XLA Ops:
  7.2 58.0 %all-gather.5.cloned.1.call-start = ((), (), s32[]{:S(2)}) async-start(), calls=%async_computation.2 | async-start | bytes 1658880 | tf_op jit(solution)/shard_map/all_gather | solution.py:931
  16.1 15.4 %collective-permute-start.2 = (bf16[48,1792]{1,0:T(8,128)(2,1)S(1)}, bf16[48,1792]{1,0:T(8,128)(2,1)S(1)}, u32[]{:S(2)}, u32[]{:S(2)}) collective-permute-start(bf16[48,1792]{1,0:T(8,128)(2,1)S(1)} %pad_maximum_fusion.9), channel_id=1, source_target_pairs={{0,8},{4,12},{8,0},{12,4},{1,9},{5,13},{9,1},{13,5},{2,10},{6,14},... | collective-permute-start | bytes 516104 | tf_op jit(solution)/shard_map/ppermute | solution.py:845
  31.5 239.0 %reduce-scatter.2.cloned.1.call-start = ((), (), s32[]{:S(2)}) async-start(), calls=%async_computation.1 | async-start | bytes 1658880 | tf_op jit(solution)/shard_map/reduce_scatter | solution.py:910
  44.5 17.0 %collective-permute-start.10 = (bf16[144,1152]{1,0:T(8,128)(2,1)S(1)}, bf16[144,1152]{1,0:T(8,128)(2,1)S(1)}, u32[]{:S(2)}, u32[]{:S(2)}) collective-permute-start(bf16[144,1152]{1,0:T(8,128)(2,1)S(1)} %slice.88.refs_0_), channel_id=1, source_target_pairs={{0,2},{1,3},{2,0},{3,1},{4,6},{5,7},{6,4},{7,5},{8,10},{9,11},{10,... | collective-permute-start | bytes 995336 | tf_op jit(solution)/shard_map/ppermute | solution.py:849
  46.1 15.4 %collective-permute-start.11 = (bf16[144,1152]{1,0:T(8,128)(2,1)S(1)}, bf16[144,1152]{1,0:T(8,128)(2,1)S(1)}, u32[]{:S(2)}, u32[]{:S(2)}) collective-permute-start(bf16[144,1152]{1,0:T(8,128)(2,1)S(1)} %slice.88.refs_0_), channel_id=1, source_target_pairs={{0,3},{1,2},{2,1},{3,0},{4,7},{5,6},{6,5},{7,4},{8,11},{9,10},{10,... | collective-permute-start | bytes 995336 | tf_op jit(solution)/shard_map/ppermute | solution.py:849
  46.8 15.9 %collective-permute-start.9 = (bf16[144,1152]{1,0:T(8,128)(2,1)S(1)}, bf16[144,1152]{1,0:T(8,128)(2,1)S(1)}, u32[]{:S(2)}, u32[]{:S(2)}) collective-permute-start(bf16[144,1152]{1,0:T(8,128)(2,1)S(1)} %slice.88.refs_0_), channel_id=1, source_target_pairs={{0,1},{1,0},{2,3},{3,2},{4,5},{5,4},{6,7},{7,6},{8,9},{9,8},{10,11... | collective-permute-start | bytes 995336 | tf_op jit(solution)/shard_map/ppermute | solution.py:849
  66.4 28.4 %collective-permute-start.6 = (bf16[720,384]{1,0:T(8,128)(2,1)S(1)}, bf16[720,384]{1,0:T(8,128)(2,1)S(1)}, u32[]{:S(2)}, u32[]{:S(2)}) collective-permute-start(bf16[720,384]{1,0:T(8,128)(2,1)S(1)} %pad_maximum_fusion.6.refs_0_), channel_id=1, source_target_pairs={{0,1},{1,0},{2,3},{3,2},{4,5},{5,4},{6,7},{7,6},{8,9},{9,8},{10,11... | collective-permute-start | bytes 1658888 | tf_op jit(solution)/shard_map/ppermute | solution.py:849
  69.5 26.1 %collective-permute-start.7 = (bf16[720,384]{1,0:T(8,128)(2,1)S(1)}, bf16[720,384]{1,0:T(8,128)(2,1)S(1)}, u32[]{:S(2)}, u32[]{:S(2)}) collective-permute-start(bf16[720,384]{1,0:T(8,128)(2,1)S(1)} %pad_maximum_fusion.6.refs_0_), channel_id=1, source_target_pairs={{0,2},{1,3},{2,0},{3,1},{4,6},{5,7},{6,4},{7,5},{8,10},{9,11},{10,... | collective-permute-start | bytes 1658888 | tf_op jit(solution)/shard_map/ppermute | solution.py:849
  70.4 25.2 %collective-permute-start.8 = (bf16[720,384]{1,0:T(8,128)(2,1)S(1)}, bf16[720,384]{1,0:T(8,128)(2,1)S(1)}, u32[]{:S(2)}, u32[]{:S(2)}) collective-permute-start(bf16[720,384]{1,0:T(8,128)(2,1)S(1)} %pad_maximum_fusion.6.refs_0_), channel_id=1, source_target_pairs={{0,3},{1,2},{2,1},{3,0},{4,7},{5,6},{6,5},{7,4},{8,11},{9,10},{10,... | collective-permute-start | bytes 1658888 | tf_op jit(solution)/shard_map/ppermute | solution.py:849
  96.7 31.5 %collective-permute-start.3 = (bf16[576,384]{1,0:T(8,128)(2,1)}, bf16[576,384]{1,0:T(8,128)(2,1)S(1)}, u32[]{:S(2)}, u32[]{:S(2)}) collective-permute-start(bf16[576,384]{1,0:T(8,128)(2,1)} %pad_maximum_fusion.7.refs_8_.refs_0_), channel_id=1, source_target_pairs={{0,1},{1,0},{2,3},{3,2},{4,5},{5,4},{6,7},{7,6},{8,9},{9,8},{10,11... | collective-permute-start | bytes 1327112 | tf_op jit(solution)/shard_map/ppermute | solution.py:849
  97.6 30.6 %collective-permute-start.4 = (bf16[576,384]{1,0:T(8,128)(2,1)}, bf16[576,384]{1,0:T(8,128)(2,1)S(1)}, u32[]{:S(2)}, u32[]{:S(2)}) collective-permute-start(bf16[576,384]{1,0:T(8,128)(2,1)} %pad_maximum_fusion.7.refs_8_.refs_0_), channel_id=1, source_target_pairs={{0,2},{1,3},{2,0},{3,1},{4,6},{5,7},{6,4},{7,5},{8,10},{9,11},{10,... | collective-permute-start | bytes 1327112 | tf_op jit(solution)/shard_map/ppermute | solution.py:849
  99.1 29.2 %collective-permute-start.5 = (bf16[576,384]{1,0:T(8,128)(2,1)}, bf16[576,384]{1,0:T(8,128)(2,1)S(1)}, u32[]{:S(2)}, u32[]{:S(2)}) collective-permute-start(bf16[576,384]{1,0:T(8,128)(2,1)} %pad_maximum_fusion.7.refs_8_.refs_0_), channel_id=1, source_target_pairs={{0,3},{1,2},{2,1},{3,0},{4,7},{5,6},{6,5},{7,4},{8,11},{9,10},{10,... | collective-permute-start | bytes 1327112 | tf_op jit(solution)/shard_map/ppermute | solution.py:849
  138.6 35.0 %collective-permute-start.28 = (bf16[4,192,384]{2,1,0:T(8,128)(2,1)S(1)}, bf16[4,192,384]{2,1,0:T(8,128)(2,1)S(1)}, u32[]{:S(2)}, u32[]{:S(2)}) collective-permute-start(bf16[4,192,384]{2,1,0:T(8,128)(2,1)S(1)} %get-tuple-element.296), channel_id=1, source_target_pairs={{0,1},{1,0},{2,3},{3,2},{4,5},{5,4},{6,7},{7,6},{8,9},{9,8},{10,11... | collective-permute-start | bytes 1769480 | tf_op jit(solution)/shard_map/ppermute | solution.py:907
  139.5 34.1 %collective-permute-start.29 = (bf16[4,192,384]{2,1,0:T(8,128)(2,1)S(1)}, bf16[4,192,384]{2,1,0:T(8,128)(2,1)S(1)}, u32[]{:S(2)}, u32[]{:S(2)}) collective-permute-start(bf16[4,192,384]{2,1,0:T(8,128)(2,1)S(1)} %get-tuple-element.295), channel_id=1, source_target_pairs={{0,2},{1,3},{2,0},{3,1},{4,6},{5,7},{6,4},{7,5},{8,10},{9,11},{10,... | collective-permute-start | bytes 1769480 | tf_op jit(solution)/shard_map/ppermute | solution.py:907
  141.0 32.6 %collective-permute-start.30 = (bf16[4,192,384]{2,1,0:T(8,128)(2,1)S(1)}, bf16[4,192,384]{2,1,0:T(8,128)(2,1)S(1)}, u32[]{:S(2)}, u32[]{:S(2)}) collective-permute-start(bf16[4,192,384]{2,1,0:T(8,128)(2,1)S(1)} %get-tuple-element.294), channel_id=1, source_target_pairs={{0,3},{1,2},{2,1},{3,0},{4,7},{5,6},{6,5},{7,4},{8,11},{9,10},{10,... | collective-permute-start | bytes 1769480 | tf_op jit(solution)/shard_map/ppermute | solution.py:907
  185.0 42.4 %collective-permute-start.39 = (bf16[4,240,384]{2,1,0:T(8,128)(2,1)}, bf16[4,240,384]{2,1,0:T(8,128)(2,1)}, u32[]{:S(2)}, u32[]{:S(2)}) collective-permute-start(bf16[4,240,384]{2,1,0:T(8,128)(2,1)} %pad_maximum_fusion.5), channel_id=1, source_target_pairs={{0,3},{1,2},{2,1},{3,0},{4,7},{5,6},{6,5},{7,4},{8,11},{9,10},{10,... | collective-permute-start | bytes 2211848 | tf_op jit(solution)/shard_map/ppermute | solution.py:907
  187.7 39.7 %collective-permute-start.38 = (bf16[4,240,384]{2,1,0:T(8,128)(2,1)}, bf16[4,240,384]{2,1,0:T(8,128)(2,1)}, u32[]{:S(2)}, u32[]{:S(2)}) collective-permute-start(bf16[4,240,384]{2,1,0:T(8,128)(2,1)} %pad_maximum_fusion.4), channel_id=1, source_target_pairs={{0,2},{1,3},{2,0},{3,1},{4,6},{5,7},{6,4},{7,5},{8,10},{9,11},{10,... | collective-permute-start | bytes 2211848 | tf_op jit(solution)/shard_map/ppermute | solution.py:907
  189.2 38.2 %collective-permute-start.37 = (bf16[4,240,384]{2,1,0:T(8,128)(2,1)}, bf16[4,240,384]{2,1,0:T(8,128)(2,1)S(1)}, u32[]{:S(2)}, u32[]{:S(2)}) collective-permute-start(bf16[4,240,384]{2,1,0:T(8,128)(2,1)} %pad_maximum_fusion.3), channel_id=1, source_target_pairs={{0,1},{1,0},{2,3},{3,2},{4,5},{5,4},{6,7},{7,6},{8,9},{9,8},{10,11... | collective-permute-start | bytes 2211848 | tf_op jit(solution)/shard_map/ppermute | solution.py:907
  231.9 76.8 %all-gather.7.cloned.1.call-start = ((), (), s32[]{:S(2)}) async-start(), calls=%async_computation.3 | async-start | bytes 2985984 | tf_op jit(solution)/shard_map/all_gather | solution.py:985
  236.9 33.6 %collective-permute-start.41 = (bf16[4,48,1664]{2,1,0:T(8,128)(2,1)}, bf16[4,48,1664]{2,1,0:T(8,128)(2,1)}, u32[]{:S(2)}, u32[]{:S(2)}) collective-permute-start(bf16[4,48,1664]{2,1,0:T(8,128)(2,1)} %get-tuple-element.288), channel_id=1, source_target_pairs={{0,1},{1,0},{2,3},{3,2},{4,5},{5,4},{6,7},{7,6},{8,9},{9,8},{10,11... | collective-permute-start | bytes 1916936 | tf_op jit(solution)/shard_map/ppermute | solution.py:907
  237.8 32.8 %collective-permute-start.42 = (bf16[4,48,1664]{2,1,0:T(8,128)(2,1)}, bf16[4,48,1664]{2,1,0:T(8,128)(2,1)}, u32[]{:S(2)}, u32[]{:S(2)}) collective-permute-start(bf16[4,48,1664]{2,1,0:T(8,128)(2,1)} %get-tuple-element.287), channel_id=1, source_target_pairs={{0,2},{1,3},{2,0},{3,1},{4,6},{5,7},{6,4},{7,5},{8,10},{9,11},{10,... | collective-permute-start | bytes 1916936 | tf_op jit(solution)/shard_map/ppermute | solution.py:907
  239.2 31.3 %collective-permute-start.43 = (bf16[4,48,1664]{2,1,0:T(8,128)(2,1)}, bf16[4,48,1664]{2,1,0:T(8,128)(2,1)}, u32[]{:S(2)}, u32[]{:S(2)}) collective-permute-start(bf16[4,48,1664]{2,1,0:T(8,128)(2,1)} %get-tuple-element.286), channel_id=1, source_target_pairs={{0,3},{1,2},{2,1},{3,0},{4,7},{5,6},{6,5},{7,4},{8,11},{9,10},{10,... | collective-permute-start | bytes 1916936 | tf_op jit(solution)/shard_map/ppermute | solution.py:907
  278.9 13.3 %collective-permute-start.45 = (bf16[48,1664]{1,0:T(8,128)(2,1)S(1)}, bf16[48,1664]{1,0:T(8,128)(2,1)S(1)}, u32[]{:S(2)}, u32[]{:S(2)}) collective-permute-start(bf16[48,1664]{1,0:T(8,128)(2,1)S(1)} %get-tuple-element.306), channel_id=1, source_target_pairs={{0,4},{4,8},{8,12},{12,0},{1,5},{5,9},{9,13},{13,1},{2,6},{6,10},{... | collective-permute-start | bytes 479240 | tf_op jit(solution)/shard_map/ppermute | solution.py:988
  278.9 13.3 %collective-permute-start.46 = (bf16[48,1664]{1,0:T(8,128)(2,1)S(1)}, bf16[48,1664]{1,0:T(8,128)(2,1)S(1)}, u32[]{:S(2)}, u32[]{:S(2)}) collective-permute-start(bf16[48,1664]{1,0:T(8,128)(2,1)S(1)} %get-tuple-element.305), channel_id=1, source_target_pairs={{0,12},{4,0},{8,4},{12,8},{1,13},{5,1},{9,5},{13,9},{2,14},{6,2},{... | collective-permute-start | bytes 479240 | tf_op jit(solution)/shard_map/ppermute | solution.py:988
  (93 other events, 768.8 us)
Sparse Core Ops, SparseCore 0:
  31.6 32.2 all-gather.4
  232.0 29.2 reduce-scatter.1
  271.2 29.1 all-gather.6

commit v2 on v1

--- a/solution.py
+++ b/solution.py
@@ -267,7 +267,7 @@
     settle(x_c)
     for r in range(0, length, R):
         hat, _ = norm_parts(x_s[r : r + R].astype(f32))
-        normed_s[r : r + R] = (hat * gain[...]).astype(bf16)
+        normed_s[r : r + R] = (hat * gain[0:1]).astype(bf16)
     settle(w_c)
     basis_c = go.start(basis_in, basis_s)
 
@@ -386,7 +386,7 @@
     act0 = (live * (x_ref[...].astype(f32) + dot(gated_ref[...], wo_ref[...]))).astype(bf16)
     act0_ref[...] = act0
     hat, _ = norm_parts(act0.astype(f32))
-    normed_ref[...] = (hat * gain_ref[...]).astype(bf16)
+    normed_ref[...] = (hat * gain_ref[1:2]).astype(bf16)
 
 
 def mixer_out(idx, rest, own_out, x, gated, gain):
@@ -494,7 +494,7 @@
         wait_all(late[1:], sem_m)
         hat, inv = norm_parts(act0_ref[...].astype(f32))
         gg_ref[...] = jnp.sum(gn[...] * hat, axis=0, keepdims=True)
-        ag = live * og_ref[...].astype(f32) + norm_back(gn[...], hat, inv, gain_ref[...])
+        ag = live * og_ref[...].astype(f32) + norm_back(gn[...], hat, inv, gain_ref[1:2])
         ag_ref[...] = ag
         branch_ref[...] = (live * ag).astype(bf16)
         for n, cols in enumerate(near_first(idx, branch_ref, half)):
@@ -531,7 +531,7 @@
 
 
 def last_kernel(idx, *refs):
-    held, (own_down, hidden_ref, act0_ref, act1_ref, wd_ref, acc, sem_d) = refs[:8], refs[8:]
+    held, (own_down, hidden_ref, act0_ref, keep_ref, hand_ref, wd_ref, acc, sem_d) = refs[:8], refs[8:]
     length, width = act0_ref.shape
     c = pl.program_id(0)
 
@@ -546,7 +546,17 @@
 
     @pl.when(c == pl.num_programs(0) - 1)
     def _():
-        act1_ref[...] = (live_rows(idx, length) * acc[...]).astype(bf16)
+        act1 = (live_rows(idx, length) * acc[...]).astype(bf16)
+
+        @pl.when(idx[2] == 0)
+        def _():
+            keep_ref[...] = act0_ref[...]
+            hand_ref[...] = act1
+
+        @pl.when(idx[2] != 0)
+        def _():
+            keep_ref[...] = act1
+            hand_ref[...] = act0_ref[...]
 
 
 def mlp_last(idx, held, own_down, hidden, act0):
@@ -557,8 +567,8 @@
         last_kernel,
         (ff // width,),
         [ANY] * 9 + [cols_of(length, width), one],
-        one,
-        sds((length, width), bf16),
+        [one, one],
+        [sds((length, width), bf16)] * 2,
         [pltpu.VMEM((ff, width), bf16), pltpu.VMEM((length, width), f32), SEMS],
         (idx, *held, own_down, hidden, act0),
         2 * length * width * ff,
@@ -759,7 +769,7 @@
     def _():
         gg_ref[...] += part
 
-    ag_ref[...] = masked_ref[...].astype(f32) + norm_back(gn, hat, inv, gain_ref[...])
+    ag_ref[...] = masked_ref[...].astype(f32) + norm_back(gn, hat, inv, gain_ref[0:1])
 
 
 def input_backward(idx, held, own_in, g_mixed, x, masked, gain):
@@ -897,8 +907,7 @@
     def both_cores(near, away):
         return total([near, lax.ppermute(away, "section", SWAP)])
 
-    def stacked(own_first, own_second, other, dtype):
-        keep = jnp.where(first, own_first, own_second).astype(dtype)
+    def stacked(keep, other, dtype):
         other = other.astype(dtype)
         both = jnp.stack([jnp.where(first, keep, other), jnp.where(first, other, keep)])
         return both[None, :, None]
@@ -916,7 +925,7 @@
     piece = jnp.concatenate([cut(own_taps, s * hl, hl, 1), own_small], 1)
     split = piece.shape[1]
     piece = jnp.concatenate([cut(piece, d * r, r, 0), cut(cut(own_in, d * r, r, 0), s * 3 * half, 3 * half, 1)], 1)
-    near = over_line(piece)
+    near, idx = lax.optimization_barrier((over_line(piece), idx))
     near_rest, near_in = near[:, :split], near[:, split:]
     plane_rest = over_plane(near_rest)
     plane_in = over_plane(near_in)
@@ -935,17 +944,16 @@
         plane_in, kernel_spectra(idx, held_rest, tie(own_taps, near_in), own_small, basis)
     )
     held_in = over_chip(plane_in)
-    gain_mix, gain_mlp = small[0:1], small[1:2]
     line_mlp = [lax.dynamic_index_in_dim(line_mlp, (z + 4 - k) % 4, 0, keepdims=False) for k in SHIFTS]
     near_up = jnp.concatenate([v[part:] for v in line_mlp], 0)
     near_down = jnp.concatenate([v[:part] for v in line_mlp], 0)
     plane_up = over_plane(near_up)
     plane_down = over_plane(near_down)
     plane_up, (normed0, mixed, qkv, sspec, conv, gated) = after(
-        plane_up, mixer_front(idx, held_in, own_in, x, gain_mix, taps, tie(spec, near_up, near_down), basis, back)
+        plane_up, mixer_front(idx, held_in, own_in, x, small, taps, tie(spec, near_up, near_down), basis, back)
     )
     held_up = over_chip(plane_up)
-    act0, normed1 = mixer_out(idx, held_up, own_out, x, gated, gain_mlp)
+    act0, normed1 = mixer_out(idx, held_up, own_out, x, gated, small)
     plane_down, (hidden, slope, near, away) = after(plane_down, mlp_up(idx, held_up, own_up, og, normed1))
     held_down = over_chip(plane_down)
 
@@ -955,7 +963,7 @@
     got_down, (ag1, branch0, g_gain_mlp, near, away, near_out, away_out) = after(
         got_down,
         mlp_down(
-            idx, held_up, held_down, own_up, own_down, og, act0, normed1, tie(slope, *sent_down), gated, gain_mlp
+            idx, held_up, held_down, own_up, own_down, og, act0, normed1, tie(slope, *sent_down), gated, small
         ),
     )
     h_up = both_cores(near, away).reshape(4, part, ff // 2)
@@ -976,11 +984,11 @@
     h_mix = both_cores(near, away).reshape(4, 4, r, 3 * half + hl)
     sent_mix = [lax.dynamic_index_in_dim(h_mix, d ^ e, 1, keepdims=False) for e in range(4)]
     got_mix = to_plane(sent_mix)
-    ag0, g_gain_mix = input_backward(idx, held_in, own_in, tie(g_mixed, u_mlp, *sent_mix), x, branch0, gain_mix)
-    act1 = mlp_last(idx, held_down, own_down, hidden, tie(act0, ag0))
+    ag0, g_gain_mix = input_backward(idx, held_in, own_in, tie(g_mixed, u_mlp, *sent_mix), x, branch0, small)
+    keep_act, hand_act = mlp_last(idx, held_down, own_down, hidden, tie(act0, ag0))
     tiny = jnp.concatenate([g_gain_mix, g_gain_mlp, g_taps], 0)
     tiny += lax.ppermute(tiny, "section", SWAP)
-    swapped = jnp.concatenate([jnp.where(first, act1, act0), jnp.where(first, ag1, ag0).astype(bf16)], 0)
+    swapped = jnp.concatenate([hand_act, jnp.where(first, ag1, ag0).astype(bf16)], 0)
     (*got_mix, p_mlp), (ag0, tiny, swapped) = after([*got_mix, p_mlp], [ag0, tiny, swapped])
     all_mlp = lax.all_gather(p_mlp, ("dp", "section"), axis=0)
     u_mix = total(got_mix)
@@ -991,18 +999,17 @@
     tiny += lax.ppermute(tiny, "dp", flip(2))
     ag0_late = tie(ag0, *sent_line)
     swapped = lax.ppermute(swapped, "section", SWAP)
-    out_act = stacked(act0, act1, swapped[:length], bf16)
-    out_ag = stacked(ag0_late, ag1, swapped[length:], f32)
+    out_act = stacked(keep_act, swapped[:length], bf16)
+    out_ag = stacked(jnp.where(first, ag0_late, ag1), swapped[length:], f32)
     got_line, (tiny, out_act, out_ag) = after(got_line, [tiny, out_act, out_ag])
     g_up, g_down, g_out = unpack(unpack_mlp_kernel, idx, [all_mlp], [(part, ff), (4 * part, width), (part, width)])
     p_mix = total(got_line)
     plane_mix = over_plane(p_mix)
     tiny = tie(tiny, p_mix)
     tiny += lax.ppermute(tiny, "chan", flip(1))
-    plane_mix, (tiny,) = after(plane_mix, [tiny])
+    plane_mix, (tiny, g_up, g_down, g_out) = after(plane_mix, [tiny, g_up, g_down, g_out])
     got_tiny = [lax.ppermute(tiny, "chan", flip(2))]
-    held_mix, (g_up, g_down, g_out) = after(over_chip(plane_mix), [g_up, g_down, g_out])
-    g_in, g_kern = unpack(unpack_mix_kernel, idx, held_mix, [(part, 3 * width), (part, length)])
+    g_in, g_kern = unpack(unpack_mix_kernel, idx, over_chip(plane_mix), [(part, 3 * width), (part, length)])
     got_tiny, (g_in, g_kern) = after(got_tiny, [g_in, g_kern])
     tiny += got_tiny[0]
 

time: 331 us -> 328 us (level)
  transfers between devices with their start and end apart: 63 -> 63, of which waited for: 15 -> 14; matrix products, arithmetic and copies ran while one was open for 12% -> 11% of each run, Pallas kernels for 49% -> 50%
where the time goes in v2:
time: 328 us; the launch traced here: 324 us
  Pallas kernels  162 us (49%)
  starting transfers between devices  49 us (15%)
  waiting for transfers between devices  46.3 us (14%)
  other arithmetic  32.6 us (10%)
  local copies, waits for them, and re-layouts  18.6 us (6%)
  between operations  15.1 us (5%)
    pallas_call x10, Pallas kernels, call(): pl.pallas_call(kernel, grid_spec=spec, out_shape=out_shape, compiler_para...  162 us
    ppermute x15, starting transfers between devices, over_plane(): return [near] + [lax.ppermute(near, 'dp', flip(e)) for e in (1, 2, 3)]  18.1 us
    convert_element_type x8, other arithmetic, total(): return out.astype(bf16)  13.8 us
    ppermute x15, waiting for transfers between devices, over_plane(): return [near] + [lax.ppermute(near, 'dp', flip(e)) for e in (1, 2, 3)]  13.1 us
    ppermute x4, waiting for transfers between devices, both_cores(): return total([near, lax.ppermute(away, 'section', SWAP)])  12 us
    ppermute x9, starting transfers between devices, to_plane(): lax.ppermute(parts[e], 'dp', flip(e))  10.5 us
    ppermute x3, waiting for transfers between devices, over_line(): lax.ppermute(piece, 'chan', shift(k))  8.87 us
  transfers between devices with their start and end apart: 63, of which 14 were waited for; matrix products, arithmetic and copies ran while one was open for 11% of the time, Pallas kernels for 50%

profile of v2, /device:TPU:0, one launch (start us, length us, event | category | flops | bytes accessed | tf_op | source)
XLA Modules:
  0.0 323.5 jit_solution(3030129951070791253)
XLA Ops:
  10.9 3.1 collective-permute-start
  23.5 7.9 %collective-permute-done.2 = bf16[48,1792]{1,0:T(8,128)(2,1)S(1)} collective-permute-done((bf16[48,1792]{1,0:T(8,128)(2,1)S(1)}, bf16[48,1792]{1,0:T(8,128)(2,1)S(1)}, u32[]{:S(2)}, u32[]{:S(2)}) %collective-permute-start.2) | collective-permute-done | bytes 172064 | tf_op jit(solution)/shard_map/ppermute | solution.py:855
  35.2 4.0 %collective-permute-done.12.refs_1_ = bf16[144,640]{1,0:T(8,128)(2,1)S(1)} collective-permute-done((bf16[144,640]{1,0:T(8,128)(2,1)S(1)}, bf16[144,640]{1,0:T(8,128)(2,1)S(1)}, u32[]{:S(2)}, u32[]{:S(2)}) %collective-permute-start.12) | collective-permute-done | bytes 184352 | tf_op jit(solution)/shard_map/ppermute | solution.py:859
  39.2 4.2 %collective-permute-done.13.refs_2_ = bf16[144,640]{1,0:T(8,128)(2,1)S(1)} collective-permute-done((bf16[144,640]{1,0:T(8,128)(2,1)S(1)}, bf16[144,640]{1,0:T(8,128)(2,1)S(1)}, u32[]{:S(2)}, u32[]{:S(2)}) %collective-permute-start.13) | collective-permute-done | bytes 184352 | tf_op jit(solution)/shard_map/ppermute | solution.py:859
  48.2 9.4 %shard_map.204 = (bf16[2048,768]{1,0:T(8,128)(2,1)}, f32[8,768]{1,0:T(8,128)}, f32[8,2304]{1,0:T(8,128)}) custom-call(s32[4]{0:T(128)} %pad_add_fusion.idx, bf16[144,640]{1,0:T(8,128)(2,1)} %copy-done.27, bf16[144,640]{1,0:T(8,128)(2,1)} %copy-done.45, bf16[144,640]{1,0:T(8,128)(2,1)} %copy-done.46, bf16[144,640]{1,0:T(8,128)(2,1)} %copy-done.47, ...), custom_call_target="tpu_custom_call" | custom-call | flops 3221225472 | bytes 8912896 | tf_op jit(solution)/shard_map/pallas_call | solution.py:48
  57.6 3.3 %collective-permute-done.10.refs_2_ = bf16[144,1152]{1,0:T(8,128)(2,1)S(1)} collective-permute-done((bf16[144,1152]{1,0:T(8,128)(2,1)S(1)}, bf16[144,1152]{1,0:T(8,128)(2,1)S(1)}, u32[]{:S(2)}, u32[]{:S(2)}) %collective-permute-start.10) | collective-permute-done | bytes 331808 | tf_op jit(solution)/shard_map/ppermute | solution.py:859
  70.0 22.8 %shard_map.205 = (bf16[1024,768]{1,0:T(8,128)(2,1)}, bf16[3,1024,768]{2,1,0:T(8,128)(2,1)}, bf16[3,1024,768]{2,1,0:T(8,128)(2,1)}, bf16[2048,768]{1,0:T(8,128)(2...) custom-call(s32[4]{0:T(128)} %pad_add_fusion.idx, bf16[144,1152]{1,0:T(8,128)(2,1)} %copy-done.24, ...), custom_call_target="tpu_custom_call" | custom-call | flops 10066329600 | bytes 37093376 | tf_op jit(solution)/shard_map/pallas_call | solution.py:48
  99.1 7.0 %shard_map.206 = (bf16[1024,768]{1,0:T(8,128)(2,1)}, bf16[1024,768]{1,0:T(8,128)(2,1)}) custom-call(s32[4]{0:T(128)} %pad_add_fusion.idx, bf16[720,384]{1,0:T(8,128)(2,1)} %copy-done.7, bf16[720,384]{1,0:T(8,128)(2,1)} %copy-done.16, bf16[720,384]{1,0:T(8,128)(2,1)} %copy-done.17, bf16[720,384]{1,0:T(8,128)(2,1)} %copy-done.18, bf16[720,384]{1,0:T(8,128)(2,1)} %copy-done.19, ...), custom_call_target="tpu_custom_call" | custom-call | flops 1207959552 | bytes 7471104 | tf_op jit(solution)/shard_map/pallas_call | solution.py:48
  106.1 19.8 %shard_map.207 = (bf16[1024,3072]{1,0:T(8,128)(2,1)}, bf16[1024,3072]{1,0:T(8,128)(2,1)}, bf16[3072,384]{1,0:T(8,128)(2,1)}, bf16[3072,384]{1,0:T(8,128)(2,1)}) custom-call(s32[4]{0:T(128)} %pad_add_fusion.idx, bf16[720,384]{1,0:T(8,128)(2,1)} %copy-done.7, bf16[720,384]{1,0:T(8,128)(2,1)} %copy-done.16, bf16[720,384]{1,0:T(8,128)(2,1)} %copy-done.17, ...), custom_call_target="tpu_custom_call" | custom-call | flops 9663676416 | bytes 25165824 | tf_op jit(solution)/shard_map/pallas_call | solution.py:48
  127.9 6.2 %collective-permute-done.27 = bf16[3072,384]{1,0:T(8,128)(2,1)S(1)} collective-permute-done((bf16[3072,384]{1,0:T(8,128)(2,1)}, bf16[3072,384]{1,0:T(8,128)(2,1)S(1)}, u32[]{:S(2)}, u32[]{:S(2)}) %collective-permute-start.27) | collective-permute-done | bytes 2359328 | tf_op jit(solution)/shard_map/ppermute | solution.py:908
  140.4 31.4 %shard_map.208 = (f32[1024,768]{1,0:T(8,128)}, bf16[1024,768]{1,0:T(8,128)(2,1)}, f32[1,768]{1,0:T(1,128)}, bf16[768,1536]{1,0:T(8,128)(2,1)}, bf16[768,1536]{1,...) custom-call(s32[4]{0:T(128)} %pad_add_fusion.idx, bf16[720,384]{1,0:T(8,128)(2,1)} %copy-done.7, ...), custom_call_target="tpu_custom_call" | custom-call | flops 14495514624 | bytes 31457280 | tf_op jit(solution)/shard_map/pallas_call | solution.py:48
  173.1 5.1 %collective-permute-done.36 = bf16[768,384]{1,0:T(8,128)(2,1)S(1)} collective-permute-done((bf16[768,384]{1,0:T(8,128)(2,1)}, bf16[768,384]{1,0:T(8,128)(2,1)S(1)}, u32[]{:S(2)}, u32[]{:S(2)}) %collective-permute-start.36) | collective-permute-done | bytes 589856 | tf_op jit(solution)/shard_map/ppermute | solution.py:908
  188.7 37.0 %shard_map.209 = (bf16[3,1024,768]{2,1,0:T(8,128)(2,1)}, bf16[768,1664]{1,0:T(8,128)(2,1)}, bf16[768,1664]{1,0:T(8,128)(2,1)}, f32[9,768]{1,0:T(8,128)}) custom-call(s32[4]{0:T(128)} %pad_add_fusion.idx, bf16[720,384]{1,0:T(8,128)(2,1)} %copy-done.7, bf16[720,384]{1,0:T(8,128)(2,1)} %copy-done.16, bf16[720,384]{1,0:T(8,128)(2,1)} %copy-done.17, ...), custom_call_target="tpu_custom_call" | custom-call | flops 14495514624 | bytes 48103424 | tf_op jit(solution)/shard_map/pallas_call | solution.py:48
  231.1 2.4 add_convert_fusion
  238.6 12.2 %shard_map.210 = (f32[1024,768]{1,0:T(8,128)}, f32[1,768]{1,0:T(1,128)}) custom-call(s32[4]{0:T(128)} %pad_add_fusion.idx, bf16[144,1152]{1,0:T(8,128)(2,1)} %copy-done.24, bf16[144,1152]{1,0:T(8,128)(2,1)} %copy-done.44, bf16[144,1152]{1,0:T(8,128)(2,1)} %copy-done.42, bf16[144,1152]{1,0:T(8,128)(2,1)} %copy-done.43, ...), custom_call_target="tpu_custom_call" | custom-call | flops 3623878656 | bytes 14548992 | tf_op jit(solution)/shard_map/pallas_call | solution.py:48
  251.7 13.8 %shard_map.211 = (bf16[1024,768]{1,0:T(8,128)(2,1)}, bf16[1024,768]{1,0:T(8,128)(2,1)}) custom-call(s32[4]{0:T(128)} %pad_add_fusion.idx, bf16[576,384]{1,0:T(8,128)(2,1)} %copy-done.23, bf16[576,384]{1,0:T(8,128)(2,1)} %copy-done.37, bf16[576,384]{1,0:T(8,128)(2,1)} %copy-done.38, bf16[576,384]{1,0:T(8,128)(2,1)} %copy-done.39, ...), custom_call_target="tpu_custom_call" | custom-call | flops 4831838208 | bytes 14155776 | tf_op jit(solution)/shard_map/pallas_call | solution.py:48
  272.2 3.2 collective-permute-done.48
  277.9 2.9 collective-permute-start.46
  283.0 3.1 maximum_bitcast_fusion
  289.7 4.1 %collective-permute-done.47 = bf16[48,1664]{1,0:T(8,128)(2,1)S(1)} collective-permute-done((bf16[48,1664]{1,0:T(8,128)(2,1)S(1)}, bf16[48,1664]{1,0:T(8,128)(2,1)S(1)}, u32[]{:S(2)}, u32[]{:S(2)}) %collective-permute-start.47) | collective-permute-done | bytes 159776 | tf_op jit(solution)/shard_map/ppermute | solution.py:996
  297.5 4.1 %collective-permute-done.54 = f32[11,768]{1,0:T(8,128)S(1)} collective-permute-done((f32[11,768]{1,0:T(8,128)S(1)}, f32[11,768]{1,0:T(8,128)S(1)}, u32[]{:S(2)}, u32[]{:S(2)}) %collective-permute-start.54) | collective-permute-done | bytes 33824 | tf_op jit(solution)/shard_map/ppermute | solution.py:1009
  301.6 4.9 %shard_map.212 = (f32[192,3072]{1,0:T(8,128)}, f32[768,768]{1,0:T(8,128)}, f32[192,768]{1,0:T(8,128)}) custom-call(s32[4]{0:T(128)} %pad_add_fusion.idx, bf16[8,432,384]{2,1,0:T(8,128)(2,1)} %bitcast.109), custom_call_target="tpu_custom_call" | custom-call | bytes 7962624 | tf_op jit(solution)/shard_map/pallas_call | solution.py:48
  307.7 2.5 collective-permute-start.55
  311.6 3.7 %shard_map.213 = (f32[192,2304]{1,0:T(8,128)}, f32[192,1024]{1,0:T(8,128)}) custom-call(s32[4]{0:T(128)} %pad_add_fusion.idx, bf16[48,1664]{1,0:T(8,128)(2,1)} %copy-done.10, bf16[48,1664]{1,0:T(8,128)(2,1)} %copy-done.28, bf16[48,1664]{1,0:T(8,128)(2,1)} %copy-done.29, bf16[48,1664]{1,0:T(8,128)(2,1)} %copy-done.30, bf16[48,1664]{1,0:T(8,128)(2,1)} %copy-done.31, ...), custom_call_target="tpu_custom_call" | custom-call | bytes 3833856 | tf_op jit(solution)/shard_map/pallas_call | solution.py:48
  (274 shorter events, 90.2 us)
Async XLA Ops:
  7.2 56.7 %all-gather.5.cloned.1.call-start = ((), (), s32[]{:S(2)}) async-start(), calls=%async_computation.2 | async-start | bytes 1658880 | tf_op jit(solution)/shard_map/all_gather | solution.py:940
  16.1 15.4 %collective-permute-start.2 = (bf16[48,1792]{1,0:T(8,128)(2,1)S(1)}, bf16[48,1792]{1,0:T(8,128)(2,1)S(1)}, u32[]{:S(2)}, u32[]{:S(2)}) collective-permute-start(bf16[48,1792]{1,0:T(8,128)(2,1)S(1)} %pad_maximum_fusion.10), channel_id=1, source_target_pairs={{0,8},{4,12},{8,0},{12,4},{1,9},{5,13},{9,1},{13,5},{2,10},{6,14},... | collective-permute-start | bytes 516104 | tf_op jit(solution)/shard_map/ppermute | solution.py:855
  31.5 237.3 %reduce-scatter.2.cloned.1.call-start = ((), (), s32[]{:S(2)}) async-start(), calls=%async_computation.1 | async-start | bytes 1658880 | tf_op jit(solution)/shard_map/reduce_scatter | solution.py:919
  44.0 17.0 %collective-permute-start.10 = (bf16[144,1152]{1,0:T(8,128)(2,1)S(1)}, bf16[144,1152]{1,0:T(8,128)(2,1)S(1)}, u32[]{:S(2)}, u32[]{:S(2)}) collective-permute-start(bf16[144,1152]{1,0:T(8,128)(2,1)S(1)} %slice.72.refs_0_), channel_id=1, source_target_pairs={{0,2},{1,3},{2,0},{3,1},{4,6},{5,7},{6,4},{7,5},{8,10},{9,11},{10,... | collective-permute-start | bytes 995336 | tf_op jit(solution)/shard_map/ppermute | solution.py:859
  45.5 15.4 %collective-permute-start.11 = (bf16[144,1152]{1,0:T(8,128)(2,1)S(1)}, bf16[144,1152]{1,0:T(8,128)(2,1)S(1)}, u32[]{:S(2)}, u32[]{:S(2)}) collective-permute-start(bf16[144,1152]{1,0:T(8,128)(2,1)S(1)} %slice.72.refs_0_), channel_id=1, source_target_pairs={{0,3},{1,2},{2,1},{3,0},{4,7},{5,6},{6,5},{7,4},{8,11},{9,10},{10,... | collective-permute-start | bytes 995336 | tf_op jit(solution)/shard_map/ppermute | solution.py:859
  46.2 15.9 %collective-permute-start.9 = (bf16[144,1152]{1,0:T(8,128)(2,1)S(1)}, bf16[144,1152]{1,0:T(8,128)(2,1)S(1)}, u32[]{:S(2)}, u32[]{:S(2)}) collective-permute-start(bf16[144,1152]{1,0:T(8,128)(2,1)S(1)} %slice.72.refs_0_), channel_id=1, source_target_pairs={{0,1},{1,0},{2,3},{3,2},{4,5},{5,4},{6,7},{7,6},{8,9},{9,8},{10,11... | collective-permute-start | bytes 995336 | tf_op jit(solution)/shard_map/ppermute | solution.py:859
  65.2 27.7 %collective-permute-start.6 = (bf16[720,384]{1,0:T(8,128)(2,1)S(1)}, bf16[720,384]{1,0:T(8,128)(2,1)S(1)}, u32[]{:S(2)}, u32[]{:S(2)}) collective-permute-start(bf16[720,384]{1,0:T(8,128)(2,1)S(1)} %pad_maximum_fusion.6.refs_0_), channel_id=1, source_target_pairs={{0,1},{1,0},{2,3},{3,2},{4,5},{5,4},{6,7},{7,6},{8,9},{9,8},{10,11... | collective-permute-start | bytes 1658888 | tf_op jit(solution)/shard_map/ppermute | solution.py:859
  67.9 25.2 %collective-permute-start.7 = (bf16[720,384]{1,0:T(8,128)(2,1)S(1)}, bf16[720,384]{1,0:T(8,128)(2,1)S(1)}, u32[]{:S(2)}, u32[]{:S(2)}) collective-permute-start(bf16[720,384]{1,0:T(8,128)(2,1)S(1)} %pad_maximum_fusion.6.refs_0_), channel_id=1, source_target_pairs={{0,2},{1,3},{2,0},{3,1},{4,6},{5,7},{6,4},{7,5},{8,10},{9,11},{10,... | collective-permute-start | bytes 1658888 | tf_op jit(solution)/shard_map/ppermute | solution.py:859
  69.4 23.7 %collective-permute-start.8 = (bf16[720,384]{1,0:T(8,128)(2,1)S(1)}, bf16[720,384]{1,0:T(8,128)(2,1)S(1)}, u32[]{:S(2)}, u32[]{:S(2)}) collective-permute-start(bf16[720,384]{1,0:T(8,128)(2,1)S(1)} %pad_maximum_fusion.6.refs_0_), channel_id=1, source_target_pairs={{0,3},{1,2},{2,1},{3,0},{4,7},{5,6},{6,5},{7,4},{8,11},{9,10},{10,... | collective-permute-start | bytes 1658888 | tf_op jit(solution)/shard_map/ppermute | solution.py:859
  94.2 31.7 %collective-permute-start.3 = (bf16[576,384]{1,0:T(8,128)(2,1)S(1)}, bf16[576,384]{1,0:T(8,128)(2,1)S(1)}, u32[]{:S(2)}, u32[]{:S(2)}) collective-permute-start(bf16[576,384]{1,0:T(8,128)(2,1)S(1)} %pad_maximum_fusion.8.refs_8_.refs_0_), channel_id=1, source_target_pairs={{0,1},{1,0},{2,3},{3,2},{4,5},{5,4},{6,7},{7,6},{8,9},{9,8},{10,11... | collective-permute-start | bytes 1327112 | tf_op jit(solution)/shard_map/ppermute | solution.py:859
  95.4 30.5 %collective-permute-start.4 = (bf16[576,384]{1,0:T(8,128)(2,1)S(1)}, bf16[576,384]{1,0:T(8,128)(2,1)S(1)}, u32[]{:S(2)}, u32[]{:S(2)}) collective-permute-start(bf16[576,384]{1,0:T(8,128)(2,1)S(1)} %pad_maximum_fusion.8.refs_8_.refs_0_), channel_id=1, source_target_pairs={{0,2},{1,3},{2,0},{3,1},{4,6},{5,7},{6,4},{7,5},{8,10},{9,11},{10,... | collective-permute-start | bytes 1327112 | tf_op jit(solution)/shard_map/ppermute | solution.py:859
  96.9 29.0 %collective-permute-start.5 = (bf16[576,384]{1,0:T(8,128)(2,1)S(1)}, bf16[576,384]{1,0:T(8,128)(2,1)S(1)}, u32[]{:S(2)}, u32[]{:S(2)}) collective-permute-start(bf16[576,384]{1,0:T(8,128)(2,1)S(1)} %pad_maximum_fusion.8.refs_8_.refs_0_), channel_id=1, source_target_pairs={{0,3},{1,2},{2,1},{3,0},{4,7},{5,6},{6,5},{7,4},{8,11},{9,10},{10,... | collective-permute-start | bytes 1327112 | tf_op jit(solution)/shard_map/ppermute | solution.py:859
  136.8 35.0 %collective-permute-start.28 = (bf16[4,192,384]{2,1,0:T(8,128)(2,1)S(1)}, bf16[4,192,384]{2,1,0:T(8,128)(2,1)S(1)}, u32[]{:S(2)}, u32[]{:S(2)}) collective-permute-start(bf16[4,192,384]{2,1,0:T(8,128)(2,1)S(1)} %get-tuple-element.288), channel_id=1, source_target_pairs={{0,1},{1,0},{2,3},{3,2},{4,5},{5,4},{6,7},{7,6},{8,9},{9,8},{10,11... | collective-permute-start | bytes 1769480 | tf_op jit(solution)/shard_map/ppermute | solution.py:916
  137.8 34.1 %collective-permute-start.29 = (bf16[4,192,384]{2,1,0:T(8,128)(2,1)S(1)}, bf16[4,192,384]{2,1,0:T(8,128)(2,1)S(1)}, u32[]{:S(2)}, u32[]{:S(2)}) collective-permute-start(bf16[4,192,384]{2,1,0:T(8,128)(2,1)S(1)} %get-tuple-element.287), channel_id=1, source_target_pairs={{0,2},{1,3},{2,0},{3,1},{4,6},{5,7},{6,4},{7,5},{8,10},{9,11},{10,... | collective-permute-start | bytes 1769480 | tf_op jit(solution)/shard_map/ppermute | solution.py:916
  139.2 32.6 %collective-permute-start.30 = (bf16[4,192,384]{2,1,0:T(8,128)(2,1)S(1)}, bf16[4,192,384]{2,1,0:T(8,128)(2,1)S(1)}, u32[]{:S(2)}, u32[]{:S(2)}) collective-permute-start(bf16[4,192,384]{2,1,0:T(8,128)(2,1)S(1)} %get-tuple-element.286), channel_id=1, source_target_pairs={{0,3},{1,2},{2,1},{3,0},{4,7},{5,6},{6,5},{7,4},{8,11},{9,10},{10,... | collective-permute-start | bytes 1769480 | tf_op jit(solution)/shard_map/ppermute | solution.py:916
  183.2 42.5 %collective-permute-start.39 = (bf16[4,240,384]{2,1,0:T(8,128)(2,1)}, bf16[4,240,384]{2,1,0:T(8,128)(2,1)}, u32[]{:S(2)}, u32[]{:S(2)}) collective-permute-start(bf16[4,240,384]{2,1,0:T(8,128)(2,1)} %pad_maximum_fusion.5), channel_id=1, source_target_pairs={{0,3},{1,2},{2,1},{3,0},{4,7},{5,6},{6,5},{7,4},{8,11},{9,10},{10,... | collective-permute-start | bytes 2211848 | tf_op jit(solution)/shard_map/ppermute | solution.py:916
  185.9 39.8 %collective-permute-start.38 = (bf16[4,240,384]{2,1,0:T(8,128)(2,1)}, bf16[4,240,384]{2,1,0:T(8,128)(2,1)}, u32[]{:S(2)}, u32[]{:S(2)}) collective-permute-start(bf16[4,240,384]{2,1,0:T(8,128)(2,1)} %pad_maximum_fusion.4), channel_id=1, source_target_pairs={{0,2},{1,3},{2,0},{3,1},{4,6},{5,7},{6,4},{7,5},{8,10},{9,11},{10,... | collective-permute-start | bytes 2211848 | tf_op jit(solution)/shard_map/ppermute | solution.py:916
  187.4 38.3 %collective-permute-start.37 = (bf16[4,240,384]{2,1,0:T(8,128)(2,1)}, bf16[4,240,384]{2,1,0:T(8,128)(2,1)S(1)}, u32[]{:S(2)}, u32[]{:S(2)}) collective-permute-start(bf16[4,240,384]{2,1,0:T(8,128)(2,1)} %pad_maximum_fusion.3), channel_id=1, source_target_pairs={{0,1},{1,0},{2,3},{3,2},{4,5},{5,4},{6,7},{7,6},{8,9},{9,8},{10,11... | collective-permute-start | bytes 2211848 | tf_op jit(solution)/shard_map/ppermute | solution.py:916
  230.2 71.4 %all-gather.7.cloned.1.call-start = ((), (), s32[]{:S(2)}) async-start(), calls=%async_computation.3 | async-start | bytes 2985984 | tf_op jit(solution)/shard_map/all_gather | solution.py:993
  235.1 33.7 %collective-permute-start.41 = (bf16[4,48,1664]{2,1,0:T(8,128)(2,1)}, bf16[4,48,1664]{2,1,0:T(8,128)(2,1)}, u32[]{:S(2)}, u32[]{:S(2)}) collective-permute-start(bf16[4,48,1664]{2,1,0:T(8,128)(2,1)} %get-tuple-element.280), channel_id=1, source_target_pairs={{0,1},{1,0},{2,3},{3,2},{4,5},{5,4},{6,7},{7,6},{8,9},{9,8},{10,11... | collective-permute-start | bytes 1916936 | tf_op jit(solution)/shard_map/ppermute | solution.py:916
  236.0 32.8 %collective-permute-start.42 = (bf16[4,48,1664]{2,1,0:T(8,128)(2,1)}, bf16[4,48,1664]{2,1,0:T(8,128)(2,1)}, u32[]{:S(2)}, u32[]{:S(2)}) collective-permute-start(bf16[4,48,1664]{2,1,0:T(8,128)(2,1)} %get-tuple-element.279), channel_id=1, source_target_pairs={{0,2},{1,3},{2,0},{3,1},{4,6},{5,7},{6,4},{7,5},{8,10},{9,11},{10,... | collective-permute-start | bytes 1916936 | tf_op jit(solution)/shard_map/ppermute | solution.py:916
  237.5 31.4 %collective-permute-start.43 = (bf16[4,48,1664]{2,1,0:T(8,128)(2,1)}, bf16[4,48,1664]{2,1,0:T(8,128)(2,1)}, u32[]{:S(2)}, u32[]{:S(2)}) collective-permute-start(bf16[4,48,1664]{2,1,0:T(8,128)(2,1)} %get-tuple-element.278), channel_id=1, source_target_pairs={{0,3},{1,2},{2,1},{3,0},{4,7},{5,6},{6,5},{7,4},{8,11},{9,10},{10,... | collective-permute-start | bytes 1916936 | tf_op jit(solution)/shard_map/ppermute | solution.py:916
  251.6 17.2 %collective-permute-start.44 = (f32[11,768]{1,0:T(8,128)S(1)}, f32[11,768]{1,0:T(8,128)S(1)}, u32[]{:S(2)}, u32[]{:S(2)}) collective-permute-start(f32[11,768]{1,0:T(8,128)S(1)} %pad_maximum_fusion.11), channel_id=1, source_target_pairs={{0,16},{16,0},{1,17},{17,1},{2,18},{18,2},{3,19},{19,3},{4,20},{20... | collective-permute-start | bytes 101384 | tf_op jit(solution)/shard_map/ppermute | solution.py:990
  280.8 13.0 %collective-permute-start.47 = (bf16[48,1664]{1,0:T(8,128)(2,1)S(1)}, bf16[48,1664]{1,0:T(8,128)(2,1)S(1)}, u32[]{:S(2)}, u32[]{:S(2)}) collective-permute-start(bf16[48,1664]{1,0:T(8,128)(2,1)S(1)} %get-tuple-element.296), channel_id=1, source_target_pairs={{0,8},{4,12},{8,0},{12,4},{1,9},{5,13},{9,1},{13,5},{2,10},{6,14},... | collective-permute-start | bytes 479240 | tf_op jit(solution)/shard_map/ppermute | solution.py:996
  (90 other events, 758.0 us)
Sparse Core Ops, SparseCore 0:
  31.6 32.2 all-gather.4
  230.3 30.6 reduce-scatter.1
  269.1 29.6 all-gather.6

commit v3 on v2

--- a/solution.py
+++ b/solution.py
@@ -988,6 +988,7 @@
     keep_act, hand_act = mlp_last(idx, held_down, own_down, hidden, tie(act0, ag0))
     tiny = jnp.concatenate([g_gain_mix, g_gain_mlp, g_taps], 0)
     tiny += lax.ppermute(tiny, "section", SWAP)
+    tiny += lax.ppermute(tiny, "dp", flip(1))
     swapped = jnp.concatenate([hand_act, jnp.where(first, ag1, ag0).astype(bf16)], 0)
     (*got_mix, p_mlp), (ag0, tiny, swapped) = after([*got_mix, p_mlp], [ag0, tiny, swapped])
     all_mlp = lax.all_gather(p_mlp, ("dp", "section"), axis=0)
@@ -995,7 +996,6 @@
     sent_line = [lax.dynamic_index_in_dim(u_mix, (z + k) % 4, 0, keepdims=False) for k in (0, *SHIFTS)]
     got_line = [sent_line[0]] + [lax.ppermute(v, "chan", shift(k)) for k, v in zip(SHIFTS, sent_line[1:])]
     tiny = tie(tiny, *sent_line)
-    tiny += lax.ppermute(tiny, "dp", flip(1))
     tiny += lax.ppermute(tiny, "dp", flip(2))
     ag0_late = tie(ag0, *sent_line)
     swapped = lax.ppermute(swapped, "section", SWAP)

time: 328 us -> 332 us (1.012)
  transfers between devices with their start and end apart: 63 -> 63, of which waited for: 14 -> 15; matrix products, arithmetic and copies ran while one was open for 11% -> 11% of each run, Pallas kernels for 50% -> 49%
where the time goes in v3:
time: 332 us; the launch traced here: 328 us
  Pallas kernels  162 us (49%)
  starting transfers between devices  51.9 us (16%)
  waiting for transfers between devices  48.5 us (15%)
  other arithmetic  32.6 us (10%)
  local copies, waits for them, and re-layouts  17.8 us (5%)
  between operations  15.1 us (5%)
    pallas_call x10, Pallas kernels, call(): pl.pallas_call(kernel, grid_spec=spec, out_shape=out_shape, compiler_para...  162 us
    ppermute x15, starting transfers between devices, over_plane(): return [near] + [lax.ppermute(near, 'dp', flip(e)) for e in (1, 2, 3)]  18.1 us
    convert_element_type x8, other arithmetic, total(): return out.astype(bf16)  13.8 us
    ppermute x15, waiting for transfers between devices, over_plane(): return [near] + [lax.ppermute(near, 'dp', flip(e)) for e in (1, 2, 3)]  13.1 us
    ppermute x4, waiting for transfers between devices, both_cores(): return total([near, lax.ppermute(away, 'section', SWAP)])  12 us
    ppermute x9, starting transfers between devices, to_plane(): lax.ppermute(parts[e], 'dp', flip(e))  10.5 us
    ppermute x3, waiting for transfers between devices, over_line(): lax.ppermute(piece, 'chan', shift(k))  8.87 us
  transfers between devices with their start and end apart: 63, of which 15 were waited for; matrix products, arithmetic and copies ran while one was open for 11% of the time, Pallas kernels for 49%

profile of v3, /device:TPU:0, one launch (start us, length us, event | category | flops | bytes accessed | tf_op | source)
XLA Modules:
  0.0 328.0 jit_solution(15674209473622072948)
XLA Ops:
  10.9 3.1 collective-permute-start
  23.5 7.9 %collective-permute-done.2 = bf16[48,1792]{1,0:T(8,128)(2,1)S(1)} collective-permute-done((bf16[48,1792]{1,0:T(8,128)(2,1)S(1)}, bf16[48,1792]{1,0:T(8,128)(2,1)S(1)}, u32[]{:S(2)}, u32[]{:S(2)}) %collective-permute-start.2) | collective-permute-done | bytes 172064 | tf_op jit(solution)/shard_map/ppermute | solution.py:855
  35.2 4.0 %collective-permute-done.12.refs_1_ = bf16[144,640]{1,0:T(8,128)(2,1)S(1)} collective-permute-done((bf16[144,640]{1,0:T(8,128)(2,1)S(1)}, bf16[144,640]{1,0:T(8,128)(2,1)S(1)}, u32[]{:S(2)}, u32[]{:S(2)}) %collective-permute-start.12) | collective-permute-done | bytes 184352 | tf_op jit(solution)/shard_map/ppermute | solution.py:859
  39.2 4.2 %collective-permute-done.13.refs_2_ = bf16[144,640]{1,0:T(8,128)(2,1)S(1)} collective-permute-done((bf16[144,640]{1,0:T(8,128)(2,1)S(1)}, bf16[144,640]{1,0:T(8,128)(2,1)S(1)}, u32[]{:S(2)}, u32[]{:S(2)}) %collective-permute-start.13) | collective-permute-done | bytes 184352 | tf_op jit(solution)/shard_map/ppermute | solution.py:859
  48.2 9.4 %shard_map.204 = (bf16[2048,768]{1,0:T(8,128)(2,1)}, f32[8,768]{1,0:T(8,128)}, f32[8,2304]{1,0:T(8,128)}) custom-call(s32[4]{0:T(128)} %pad_add_fusion.idx, bf16[144,640]{1,0:T(8,128)(2,1)} %copy-done.27, bf16[144,640]{1,0:T(8,128)(2,1)} %copy-done.45, bf16[144,640]{1,0:T(8,128)(2,1)} %copy-done.46, bf16[144,640]{1,0:T(8,128)(2,1)} %copy-done.47, ...), custom_call_target="tpu_custom_call" | custom-call | flops 3221225472 | bytes 8912896 | tf_op jit(solution)/shard_map/pallas_call | solution.py:48
  57.6 3.3 %collective-permute-done.10.refs_2_ = bf16[144,1152]{1,0:T(8,128)(2,1)S(1)} collective-permute-done((bf16[144,1152]{1,0:T(8,128)(2,1)S(1)}, bf16[144,1152]{1,0:T(8,128)(2,1)S(1)}, u32[]{:S(2)}, u32[]{:S(2)}) %collective-permute-start.10) | collective-permute-done | bytes 331808 | tf_op jit(solution)/shard_map/ppermute | solution.py:859
  70.0 22.8 %shard_map.205 = (bf16[1024,768]{1,0:T(8,128)(2,1)}, bf16[3,1024,768]{2,1,0:T(8,128)(2,1)}, bf16[3,1024,768]{2,1,0:T(8,128)(2,1)}, bf16[2048,768]{1,0:T(8,128)(2...) custom-call(s32[4]{0:T(128)} %pad_add_fusion.idx, bf16[144,1152]{1,0:T(8,128)(2,1)} %copy-done.24, ...), custom_call_target="tpu_custom_call" | custom-call | flops 10066329600 | bytes 37093376 | tf_op jit(solution)/shard_map/pallas_call | solution.py:48
  99.1 7.0 %shard_map.206 = (bf16[1024,768]{1,0:T(8,128)(2,1)}, bf16[1024,768]{1,0:T(8,128)(2,1)}) custom-call(s32[4]{0:T(128)} %pad_add_fusion.idx, bf16[720,384]{1,0:T(8,128)(2,1)} %copy-done.7, bf16[720,384]{1,0:T(8,128)(2,1)} %copy-done.16, bf16[720,384]{1,0:T(8,128)(2,1)} %copy-done.17, bf16[720,384]{1,0:T(8,128)(2,1)} %copy-done.18, bf16[720,384]{1,0:T(8,128)(2,1)} %copy-done.19, ...), custom_call_target="tpu_custom_call" | custom-call | flops 1207959552 | bytes 7471104 | tf_op jit(solution)/shard_map/pallas_call | solution.py:48
  106.1 19.8 %shard_map.207 = (bf16[1024,3072]{1,0:T(8,128)(2,1)}, bf16[1024,3072]{1,0:T(8,128)(2,1)}, bf16[3072,384]{1,0:T(8,128)(2,1)}, bf16[3072,384]{1,0:T(8,128)(2,1)}) custom-call(s32[4]{0:T(128)} %pad_add_fusion.idx, bf16[720,384]{1,0:T(8,128)(2,1)} %copy-done.7, bf16[720,384]{1,0:T(8,128)(2,1)} %copy-done.16, bf16[720,384]{1,0:T(8,128)(2,1)} %copy-done.17, ...), custom_call_target="tpu_custom_call" | custom-call | flops 9663676416 | bytes 25165824 | tf_op jit(solution)/shard_map/pallas_call | solution.py:48
  127.9 6.2 %collective-permute-done.27 = bf16[3072,384]{1,0:T(8,128)(2,1)S(1)} collective-permute-done((bf16[3072,384]{1,0:T(8,128)(2,1)}, bf16[3072,384]{1,0:T(8,128)(2,1)S(1)}, u32[]{:S(2)}, u32[]{:S(2)}) %collective-permute-start.27) | collective-permute-done | bytes 2359328 | tf_op jit(solution)/shard_map/ppermute | solution.py:908
  140.4 31.4 %shard_map.208 = (f32[1024,768]{1,0:T(8,128)}, bf16[1024,768]{1,0:T(8,128)(2,1)}, f32[1,768]{1,0:T(1,128)}, bf16[768,1536]{1,0:T(8,128)(2,1)}, bf16[768,1536]{1,...) custom-call(s32[4]{0:T(128)} %pad_add_fusion.idx, bf16[720,384]{1,0:T(8,128)(2,1)} %copy-done.7, ...), custom_call_target="tpu_custom_call" | custom-call | flops 14495514624 | bytes 31457280 | tf_op jit(solution)/shard_map/pallas_call | solution.py:48
  173.1 5.1 %collective-permute-done.36 = bf16[768,384]{1,0:T(8,128)(2,1)S(1)} collective-permute-done((bf16[768,384]{1,0:T(8,128)(2,1)}, bf16[768,384]{1,0:T(8,128)(2,1)S(1)}, u32[]{:S(2)}, u32[]{:S(2)}) %collective-permute-start.36) | collective-permute-done | bytes 589856 | tf_op jit(solution)/shard_map/ppermute | solution.py:908
  188.7 37.0 %shard_map.209 = (bf16[3,1024,768]{2,1,0:T(8,128)(2,1)}, bf16[768,1664]{1,0:T(8,128)(2,1)}, bf16[768,1664]{1,0:T(8,128)(2,1)}, f32[9,768]{1,0:T(8,128)}) custom-call(s32[4]{0:T(128)} %pad_add_fusion.idx, bf16[720,384]{1,0:T(8,128)(2,1)} %copy-done.7, bf16[720,384]{1,0:T(8,128)(2,1)} %copy-done.16, bf16[720,384]{1,0:T(8,128)(2,1)} %copy-done.17, ...), custom_call_target="tpu_custom_call" | custom-call | flops 14495514624 | bytes 48103424 | tf_op jit(solution)/shard_map/pallas_call | solution.py:48
  231.1 2.4 add_convert_fusion
  238.6 12.2 %shard_map.210 = (f32[1024,768]{1,0:T(8,128)}, f32[1,768]{1,0:T(1,128)}) custom-call(s32[4]{0:T(128)} %pad_add_fusion.idx, bf16[144,1152]{1,0:T(8,128)(2,1)} %copy-done.24, bf16[144,1152]{1,0:T(8,128)(2,1)} %copy-done.44, bf16[144,1152]{1,0:T(8,128)(2,1)} %copy-done.42, bf16[144,1152]{1,0:T(8,128)(2,1)} %copy-done.43, ...), custom_call_target="tpu_custom_call" | custom-call | flops 3623878656 | bytes 14548992 | tf_op jit(solution)/shard_map/pallas_call | solution.py:48
  251.7 13.8 %shard_map.211 = (bf16[1024,768]{1,0:T(8,128)(2,1)}, bf16[1024,768]{1,0:T(8,128)(2,1)}) custom-call(s32[4]{0:T(128)} %pad_add_fusion.idx, bf16[576,384]{1,0:T(8,128)(2,1)} %copy-done.23, bf16[576,384]{1,0:T(8,128)(2,1)} %copy-done.37, bf16[576,384]{1,0:T(8,128)(2,1)} %copy-done.38, bf16[576,384]{1,0:T(8,128)(2,1)} %copy-done.39, ...), custom_call_target="tpu_custom_call" | custom-call | flops 4831838208 | bytes 14155776 | tf_op jit(solution)/shard_map/pallas_call | solution.py:48
  275.1 3.0 collective-permute-start.47
  280.3 3.1 maximum_bitcast_fusion
  287.0 5.3 %collective-permute-done.48 = bf16[48,1664]{1,0:T(8,128)(2,1)S(1)} collective-permute-done((bf16[48,1664]{1,0:T(8,128)(2,1)S(1)}, bf16[48,1664]{1,0:T(8,128)(2,1)S(1)}, u32[]{:S(2)}, u32[]{:S(2)}) %collective-permute-start.48) | collective-permute-done | bytes 159776 | tf_op jit(solution)/shard_map/ppermute | solution.py:997
  296.0 4.1 %collective-permute-done.54 = f32[11,768]{1,0:T(8,128)S(1)} collective-permute-done((f32[11,768]{1,0:T(8,128)S(1)}, f32[11,768]{1,0:T(8,128)S(1)}, u32[]{:S(2)}, u32[]{:S(2)}) %collective-permute-start.54) | collective-permute-done | bytes 33824 | tf_op jit(solution)/shard_map/ppermute | solution.py:1009
  300.1 2.9 all-gather.7.cloned.1.call-done
  303.1 4.9 %shard_map.212 = (f32[192,3072]{1,0:T(8,128)}, f32[768,768]{1,0:T(8,128)}, f32[192,768]{1,0:T(8,128)}) custom-call(s32[4]{0:T(128)} %pad_add_fusion.idx, bf16[8,432,384]{2,1,0:T(8,128)(2,1)} %bitcast.109), custom_call_target="tpu_custom_call" | custom-call | bytes 7962624 | tf_op jit(solution)/shard_map/pallas_call | solution.py:48
  309.1 5.5 %collective-permute-start.55 = (f32[11,768]{1,0:T(8,128)S(1)}, f32[11,768]{1,0:T(8,128)S(1)}, u32[]{:S(2)}, u32[]{:S(2)}) collective-permute-start(f32[11,768]{1,0:T(8,128)S(1)} %add.236), channel_id=1, source_target_pairs={{0,8},{4,12},{8,0},{12,4},{1,9},{5,13},{9,1},{13,5},{2,10},{6,14},... | collective-permute-start | bytes 101384 | tf_op jit(solution)/shard_map/ppermute | solution.py:1011
  316.1 3.7 %shard_map.213 = (f32[192,2304]{1,0:T(8,128)}, f32[192,1024]{1,0:T(8,128)}) custom-call(s32[4]{0:T(128)} %pad_add_fusion.idx, bf16[48,1664]{1,0:T(8,128)(2,1)} %copy-done.10, bf16[48,1664]{1,0:T(8,128)(2,1)} %copy-done.28, bf16[48,1664]{1,0:T(8,128)(2,1)} %copy-done.29, bf16[48,1664]{1,0:T(8,128)(2,1)} %copy-done.30, bf16[48,1664]{1,0:T(8,128)(2,1)} %copy-done.31, ...), custom_call_target="tpu_custom_call" | custom-call | bytes 3833856 | tf_op jit(solution)/shard_map/pallas_call | solution.py:48
  (274 shorter events, 90.6 us)
Async XLA Ops:
  7.2 56.7 %all-gather.5.cloned.1.call-start = ((), (), s32[]{:S(2)}) async-start(), calls=%async_computation.2 | async-start | bytes 1658880 | tf_op jit(solution)/shard_map/all_gather | solution.py:940
  16.1 15.4 %collective-permute-start.2 = (bf16[48,1792]{1,0:T(8,128)(2,1)S(1)}, bf16[48,1792]{1,0:T(8,128)(2,1)S(1)}, u32[]{:S(2)}, u32[]{:S(2)}) collective-permute-start(bf16[48,1792]{1,0:T(8,128)(2,1)S(1)} %pad_maximum_fusion.10), channel_id=1, source_target_pairs={{0,8},{4,12},{8,0},{12,4},{1,9},{5,13},{9,1},{13,5},{2,10},{6,14},... | collective-permute-start | bytes 516104 | tf_op jit(solution)/shard_map/ppermute | solution.py:855
  31.5 238.9 %reduce-scatter.2.cloned.1.call-start = ((), (), s32[]{:S(2)}) async-start(), calls=%async_computation.1 | async-start | bytes 1658880 | tf_op jit(solution)/shard_map/reduce_scatter | solution.py:919
  44.0 17.0 %collective-permute-start.10 = (bf16[144,1152]{1,0:T(8,128)(2,1)S(1)}, bf16[144,1152]{1,0:T(8,128)(2,1)S(1)}, u32[]{:S(2)}, u32[]{:S(2)}) collective-permute-start(bf16[144,1152]{1,0:T(8,128)(2,1)S(1)} %slice.72.refs_0_), channel_id=1, source_target_pairs={{0,2},{1,3},{2,0},{3,1},{4,6},{5,7},{6,4},{7,5},{8,10},{9,11},{10,... | collective-permute-start | bytes 995336 | tf_op jit(solution)/shard_map/ppermute | solution.py:859
  45.5 15.4 %collective-permute-start.11 = (bf16[144,1152]{1,0:T(8,128)(2,1)S(1)}, bf16[144,1152]{1,0:T(8,128)(2,1)S(1)}, u32[]{:S(2)}, u32[]{:S(2)}) collective-permute-start(bf16[144,1152]{1,0:T(8,128)(2,1)S(1)} %slice.72.refs_0_), channel_id=1, source_target_pairs={{0,3},{1,2},{2,1},{3,0},{4,7},{5,6},{6,5},{7,4},{8,11},{9,10},{10,... | collective-permute-start | bytes 995336 | tf_op jit(solution)/shard_map/ppermute | solution.py:859
  46.2 15.9 %collective-permute-start.9 = (bf16[144,1152]{1,0:T(8,128)(2,1)S(1)}, bf16[144,1152]{1,0:T(8,128)(2,1)S(1)}, u32[]{:S(2)}, u32[]{:S(2)}) collective-permute-start(bf16[144,1152]{1,0:T(8,128)(2,1)S(1)} %slice.72.refs_0_), channel_id=1, source_target_pairs={{0,1},{1,0},{2,3},{3,2},{4,5},{5,4},{6,7},{7,6},{8,9},{9,8},{10,11... | collective-permute-start | bytes 995336 | tf_op jit(solution)/shard_map/ppermute | solution.py:859
  65.2 27.7 %collective-permute-start.6 = (bf16[720,384]{1,0:T(8,128)(2,1)S(1)}, bf16[720,384]{1,0:T(8,128)(2,1)S(1)}, u32[]{:S(2)}, u32[]{:S(2)}) collective-permute-start(bf16[720,384]{1,0:T(8,128)(2,1)S(1)} %pad_maximum_fusion.6.refs_0_), channel_id=1, source_target_pairs={{0,1},{1,0},{2,3},{3,2},{4,5},{5,4},{6,7},{7,6},{8,9},{9,8},{10,11... | collective-permute-start | bytes 1658888 | tf_op jit(solution)/shard_map/ppermute | solution.py:859
  67.9 25.2 %collective-permute-start.7 = (bf16[720,384]{1,0:T(8,128)(2,1)S(1)}, bf16[720,384]{1,0:T(8,128)(2,1)S(1)}, u32[]{:S(2)}, u32[]{:S(2)}) collective-permute-start(bf16[720,384]{1,0:T(8,128)(2,1)S(1)} %pad_maximum_fusion.6.refs_0_), channel_id=1, source_target_pairs={{0,2},{1,3},{2,0},{3,1},{4,6},{5,7},{6,4},{7,5},{8,10},{9,11},{10,... | collective-permute-start | bytes 1658888 | tf_op jit(solution)/shard_map/ppermute | solution.py:859
  69.4 23.7 %collective-permute-start.8 = (bf16[720,384]{1,0:T(8,128)(2,1)S(1)}, bf16[720,384]{1,0:T(8,128)(2,1)S(1)}, u32[]{:S(2)}, u32[]{:S(2)}) collective-permute-start(bf16[720,384]{1,0:T(8,128)(2,1)S(1)} %pad_maximum_fusion.6.refs_0_), channel_id=1, source_target_pairs={{0,3},{1,2},{2,1},{3,0},{4,7},{5,6},{6,5},{7,4},{8,11},{9,10},{10,... | collective-permute-start | bytes 1658888 | tf_op jit(solution)/shard_map/ppermute | solution.py:859
  94.2 31.7 %collective-permute-start.3 = (bf16[576,384]{1,0:T(8,128)(2,1)S(1)}, bf16[576,384]{1,0:T(8,128)(2,1)S(1)}, u32[]{:S(2)}, u32[]{:S(2)}) collective-permute-start(bf16[576,384]{1,0:T(8,128)(2,1)S(1)} %pad_maximum_fusion.8.refs_8_.refs_0_), channel_id=1, source_target_pairs={{0,1},{1,0},{2,3},{3,2},{4,5},{5,4},{6,7},{7,6},{8,9},{9,8},{10,11... | collective-permute-start | bytes 1327112 | tf_op jit(solution)/shard_map/ppermute | solution.py:859
  95.4 30.5 %collective-permute-start.4 = (bf16[576,384]{1,0:T(8,128)(2,1)S(1)}, bf16[576,384]{1,0:T(8,128)(2,1)S(1)}, u32[]{:S(2)}, u32[]{:S(2)}) collective-permute-start(bf16[576,384]{1,0:T(8,128)(2,1)S(1)} %pad_maximum_fusion.8.refs_8_.refs_0_), channel_id=1, source_target_pairs={{0,2},{1,3},{2,0},{3,1},{4,6},{5,7},{6,4},{7,5},{8,10},{9,11},{10,... | collective-permute-start | bytes 1327112 | tf_op jit(solution)/shard_map/ppermute | solution.py:859
  96.9 29.0 %collective-permute-start.5 = (bf16[576,384]{1,0:T(8,128)(2,1)S(1)}, bf16[576,384]{1,0:T(8,128)(2,1)S(1)}, u32[]{:S(2)}, u32[]{:S(2)}) collective-permute-start(bf16[576,384]{1,0:T(8,128)(2,1)S(1)} %pad_maximum_fusion.8.refs_8_.refs_0_), channel_id=1, source_target_pairs={{0,3},{1,2},{2,1},{3,0},{4,7},{5,6},{6,5},{7,4},{8,11},{9,10},{10,... | collective-permute-start | bytes 1327112 | tf_op jit(solution)/shard_map/ppermute | solution.py:859
  136.8 35.0 %collective-permute-start.28 = (bf16[4,192,384]{2,1,0:T(8,128)(2,1)S(1)}, bf16[4,192,384]{2,1,0:T(8,128)(2,1)S(1)}, u32[]{:S(2)}, u32[]{:S(2)}) collective-permute-start(bf16[4,192,384]{2,1,0:T(8,128)(2,1)S(1)} %get-tuple-element.288), channel_id=1, source_target_pairs={{0,1},{1,0},{2,3},{3,2},{4,5},{5,4},{6,7},{7,6},{8,9},{9,8},{10,11... | collective-permute-start | bytes 1769480 | tf_op jit(solution)/shard_map/ppermute | solution.py:916
  137.8 34.1 %collective-permute-start.29 = (bf16[4,192,384]{2,1,0:T(8,128)(2,1)S(1)}, bf16[4,192,384]{2,1,0:T(8,128)(2,1)S(1)}, u32[]{:S(2)}, u32[]{:S(2)}) collective-permute-start(bf16[4,192,384]{2,1,0:T(8,128)(2,1)S(1)} %get-tuple-element.287), channel_id=1, source_target_pairs={{0,2},{1,3},{2,0},{3,1},{4,6},{5,7},{6,4},{7,5},{8,10},{9,11},{10,... | collective-permute-start | bytes 1769480 | tf_op jit(solution)/shard_map/ppermute | solution.py:916
  139.2 32.6 %collective-permute-start.30 = (bf16[4,192,384]{2,1,0:T(8,128)(2,1)S(1)}, bf16[4,192,384]{2,1,0:T(8,128)(2,1)S(1)}, u32[]{:S(2)}, u32[]{:S(2)}) collective-permute-start(bf16[4,192,384]{2,1,0:T(8,128)(2,1)S(1)} %get-tuple-element.286), channel_id=1, source_target_pairs={{0,3},{1,2},{2,1},{3,0},{4,7},{5,6},{6,5},{7,4},{8,11},{9,10},{10,... | collective-permute-start | bytes 1769480 | tf_op jit(solution)/shard_map/ppermute | solution.py:916
  183.2 42.5 %collective-permute-start.39 = (bf16[4,240,384]{2,1,0:T(8,128)(2,1)}, bf16[4,240,384]{2,1,0:T(8,128)(2,1)}, u32[]{:S(2)}, u32[]{:S(2)}) collective-permute-start(bf16[4,240,384]{2,1,0:T(8,128)(2,1)} %pad_maximum_fusion.5), channel_id=1, source_target_pairs={{0,3},{1,2},{2,1},{3,0},{4,7},{5,6},{6,5},{7,4},{8,11},{9,10},{10,... | collective-permute-start | bytes 2211848 | tf_op jit(solution)/shard_map/ppermute | solution.py:916
  185.9 39.8 %collective-permute-start.38 = (bf16[4,240,384]{2,1,0:T(8,128)(2,1)}, bf16[4,240,384]{2,1,0:T(8,128)(2,1)}, u32[]{:S(2)}, u32[]{:S(2)}) collective-permute-start(bf16[4,240,384]{2,1,0:T(8,128)(2,1)} %pad_maximum_fusion.4), channel_id=1, source_target_pairs={{0,2},{1,3},{2,0},{3,1},{4,6},{5,7},{6,4},{7,5},{8,10},{9,11},{10,... | collective-permute-start | bytes 2211848 | tf_op jit(solution)/shard_map/ppermute | solution.py:916
  187.4 38.3 %collective-permute-start.37 = (bf16[4,240,384]{2,1,0:T(8,128)(2,1)}, bf16[4,240,384]{2,1,0:T(8,128)(2,1)S(1)}, u32[]{:S(2)}, u32[]{:S(2)}) collective-permute-start(bf16[4,240,384]{2,1,0:T(8,128)(2,1)} %pad_maximum_fusion.3), channel_id=1, source_target_pairs={{0,1},{1,0},{2,3},{3,2},{4,5},{5,4},{6,7},{7,6},{8,9},{9,8},{10,11... | collective-permute-start | bytes 2211848 | tf_op jit(solution)/shard_map/ppermute | solution.py:916
  230.2 72.9 %all-gather.7.cloned.1.call-start = ((), (), s32[]{:S(2)}) async-start(), calls=%async_computation.3 | async-start | bytes 2985984 | tf_op jit(solution)/shard_map/all_gather | solution.py:994
  235.1 35.3 %collective-permute-start.41 = (bf16[4,48,1664]{2,1,0:T(8,128)(2,1)}, bf16[4,48,1664]{2,1,0:T(8,128)(2,1)}, u32[]{:S(2)}, u32[]{:S(2)}) collective-permute-start(bf16[4,48,1664]{2,1,0:T(8,128)(2,1)} %get-tuple-element.280), channel_id=1, source_target_pairs={{0,1},{1,0},{2,3},{3,2},{4,5},{5,4},{6,7},{7,6},{8,9},{9,8},{10,11... | collective-permute-start | bytes 1916936 | tf_op jit(solution)/shard_map/ppermute | solution.py:916
  236.0 34.4 %collective-permute-start.42 = (bf16[4,48,1664]{2,1,0:T(8,128)(2,1)}, bf16[4,48,1664]{2,1,0:T(8,128)(2,1)}, u32[]{:S(2)}, u32[]{:S(2)}) collective-permute-start(bf16[4,48,1664]{2,1,0:T(8,128)(2,1)} %get-tuple-element.279), channel_id=1, source_target_pairs={{0,2},{1,3},{2,0},{3,1},{4,6},{5,7},{6,4},{7,5},{8,10},{9,11},{10,... | collective-permute-start | bytes 1916936 | tf_op jit(solution)/shard_map/ppermute | solution.py:916
  237.5 32.9 %collective-permute-start.43 = (bf16[4,48,1664]{2,1,0:T(8,128)(2,1)}, bf16[4,48,1664]{2,1,0:T(8,128)(2,1)}, u32[]{:S(2)}, u32[]{:S(2)}) collective-permute-start(bf16[4,48,1664]{2,1,0:T(8,128)(2,1)} %get-tuple-element.278), channel_id=1, source_target_pairs={{0,3},{1,2},{2,1},{3,0},{4,7},{5,6},{6,5},{7,4},{8,11},{9,10},{10,... | collective-permute-start | bytes 1916936 | tf_op jit(solution)/shard_map/ppermute | solution.py:916
  292.5 15.5 %collective-permute-start.51 = (bf16[48,1664]{1,0:T(8,128)(2,1)S(1)}, bf16[48,1664]{1,0:T(8,128)(2,1)S(1)}, u32[]{:S(2)}, u32[]{:S(2)}) collective-permute-start(bf16[48,1664]{1,0:T(8,128)(2,1)S(1)} %add_convert_fusion.7.refs_0_), channel_id=1, source_target_pairs={{0,1},{1,0},{2,3},{3,2},{4,5},{5,4},{6,7},{7,6},{8,9},{9,8},{10,11... | collective-permute-start | bytes 479240 | tf_op jit(solution)/shard_map/ppermute | solution.py:859
  293.6 14.4 %collective-permute-start.52 = (bf16[48,1664]{1,0:T(8,128)(2,1)S(1)}, bf16[48,1664]{1,0:T(8,128)(2,1)S(1)}, u32[]{:S(2)}, u32[]{:S(2)}) collective-permute-start(bf16[48,1664]{1,0:T(8,128)(2,1)S(1)} %add_convert_fusion.7.refs_0_), channel_id=1, source_target_pairs={{0,2},{1,3},{2,0},{3,1},{4,6},{5,7},{6,4},{7,5},{8,10},{9,11},{10,... | collective-permute-start | bytes 479240 | tf_op jit(solution)/shard_map/ppermute | solution.py:859
  (90 other events, 791.5 us)
Sparse Core Ops, SparseCore 0:
  31.6 32.2 all-gather.4
  230.3 30.6 reduce-scatter.1
  270.6 32.3 all-gather.6
